TPU v7x, 32 devices: a whole 2x2x4 slice. The times are simulated.
32 devices in a mesh: section: 2 (over x), ctx: 16 (over z, y, core).
Axes of the slice: x: 2, y: 2, z: 4, core: 2. Of those that a mesh axis runs over, the one named last changes fastest.
Arguments:
- inputs: bfloat16 [2, 1024, 2048], P('section', None, 'ctx'), may hold values from -6 to 6
- out_grad: bfloat16 [1024, 2048], P(None, 'ctx'), may hold values from -6 to 6
- filters: bfloat16 [2, 1024, 2048], P('section', 'ctx'), may hold values from -0.125 to 0.125
- conv_taps: float32 [2, 3, 7, 1024], P('section'), may hold values from -2.5 to 2.5
Outputs:
- in_grad: bfloat16 [2, 1024, 2048], P('section', None, 'ctx')
- filter_grad: float32 [2, 1024, 2048], P('section', 'ctx')
- tap_grad: float32 [2, 3, 7, 1024], P('section', None, None, 'ctx')
All inputs are finite; a program needn't handle non-finite values.
Results may differ from a plain program's by a relative error of at most 0.014.
Values may be sent and summed in bfloat16 or wider, within the bound.
A program may use at most 64 MiB of HBM per device.

v0:
```python
import functools
import math

import jax
import jax.numpy as jnp
import ml_dtypes
import numpy as np
from jax import lax
from jax.experimental import pallas as pl
from jax.experimental.pallas import tpu as pltpu
from jax.sharding import PartitionSpec as P

PRECISE = lax.Precision.HIGH


def shifted(block, axis, distance):
    devices = range(lax.axis_size(axis))
    route = [(i - distance, i) for i in devices if i - distance in devices]
    return lax.ppermute(block, axis, route)


def angle_table(row_count, col_count, modulus):
    row_ids = lax.broadcasted_iota(jnp.int32, (row_count, col_count), 0)
    col_ids = lax.broadcasted_iota(jnp.int32, (row_count, col_count), 1)
    product_mod = row_ids * col_ids % modulus
    angles = product_mod.astype(jnp.float32) * (2.0 * math.pi / modulus)
    return (jnp.cos(angles), jnp.sin(angles))


def make_tables(blocks_a, block_b):
    half_a = blocks_a // 2
    total_n = blocks_a * block_b
    return (
        angle_table(blocks_a, half_a, blocks_a),
        angle_table(half_a, blocks_a, blocks_a),
        angle_table(blocks_a, block_b, total_n),
        angle_table(block_b, block_b, block_b),
    )


def forward_spectrum(signal, tables):
    cos_one, sin_one = tables[0]
    cos_tw, sin_tw = tables[2]
    cos_two, sin_two = tables[3]
    channels = signal.shape[0]
    half_a = cos_one.shape[1]
    block_b = cos_two.shape[0]
    shaped = signal.reshape(channels, half_a, block_b)
    real_y = jnp.einsum("ka,cab->ckb", cos_one, shaped, precision=PRECISE)
    imag_y = -jnp.einsum("ka,cab->ckb", sin_one, shaped, precision=PRECISE)
    real_z = real_y * cos_tw + imag_y * sin_tw
    imag_z = imag_y * cos_tw - real_y * sin_tw
    real_x = jnp.einsum("ckb,mb->ckm", real_z, cos_two, precision=PRECISE) + jnp.einsum(
        "ckb,mb->ckm", imag_z, sin_two, precision=PRECISE
    )
    imag_x = jnp.einsum("ckb,mb->ckm", imag_z, cos_two, precision=PRECISE) - jnp.einsum(
        "ckb,mb->ckm", real_z, sin_two, precision=PRECISE
    )
    return (real_x, imag_x)


def inverse_signal(real_x, imag_x, tables):
    cos_one, sin_one = tables[1]
    cos_tw, sin_tw = tables[2]
    cos_two, sin_two = tables[3]
    channels = real_x.shape[0]
    half_a = cos_one.shape[0]
    block_b = cos_two.shape[0]
    total_n = cos_one.shape[1] * block_b
    real_p = jnp.einsum("ckm,mb->ckb", real_x, cos_two, precision=PRECISE) - jnp.einsum(
        "ckm,mb->ckb", imag_x, sin_two, precision=PRECISE
    )
    imag_p = jnp.einsum("ckm,mb->ckb", real_x, sin_two, precision=PRECISE) + jnp.einsum(
        "ckm,mb->ckb", imag_x, cos_two, precision=PRECISE
    )
    real_q = real_p * cos_tw - imag_p * sin_tw
    imag_q = real_p * sin_tw + imag_p * cos_tw
    summed = jnp.einsum("ak,ckb->cab", cos_one, real_q, precision=PRECISE) - jnp.einsum(
        "ak,ckb->cab", sin_one, imag_q, precision=PRECISE
    )
    return summed.reshape(channels, half_a * block_b) / total_n


def times_conj(real_a, imag_a, real_b, imag_b):
    return (real_a * real_b + imag_a * imag_b, real_a * imag_b - imag_a * real_b)


def features(padded, weights, length):
    summed = jnp.zeros((3, padded.shape[0], length), jnp.float32)
    for offset in range(7):
        window = padded[:, 6 - offset : 6 - offset + length].astype(jnp.float32)
        summed = summed + weights[:, offset, :, None] * window[None]
    return summed.astype(jnp.bfloat16)


def transposed(grad_all, weights):
    length = grad_all.shape[2]
    padded = jnp.pad(grad_all, ((0, 0), (0, 0), (0, 6)))
    summed = jnp.zeros(grad_all.shape[1:], jnp.float32)
    for offset in range(7):
        summed = summed + jnp.sum(
            weights[:, offset, :, None] * padded[:, :, offset : offset + length], axis=0
        )
    return summed


def tap_grads(padded, grad_all):
    length = grad_all.shape[2]
    per_offset = []
    for offset in range(7):
        window = padded[:, 6 - offset : 6 - offset + length].astype(jnp.float32)
        per_offset.append(jnp.sum(grad_all * window[None], axis=2))
    return jnp.stack(per_offset, axis=1)


def take_rows(array, first_ch, count, axis_num):
    return lax.dynamic_slice_in_dim(array, first_ch, count, axis_num)


def masked_write(array, update, first_ch, active, axis_num):
    previous = lax.dynamic_slice_in_dim(array, first_ch, update.shape[axis_num], axis_num)
    return lax.dynamic_update_slice_in_dim(
        array, jnp.where(active, update, previous), first_ch, axis_num
    )


def shards(inputs, out_grad, filters, conv_taps):
    x_rows = inputs[0]
    tok_dev = x_rows.shape[1]
    section_count = lax.axis_size("section")
    section_idx = lax.axis_index("section")
    ctx_idx = lax.axis_index("ctx")
    weights = conv_taps[0]
    channels = filters.shape[1]
    length = filters.shape[2]
    blocks_a = 2 * length // tok_dev
    own_taps = lax.dynamic_slice_in_dim(weights, ctx_idx * channels, channels, 2)
    prior_cols = shifted(x_rows[:, tok_dev - 6 :], "ctx", 1)
    featured_rows = features(jnp.concatenate([prior_cols, x_rows], axis=1), weights, tok_dev)
    x_chan, featured, grad_chan = (
        lax.all_to_all(x_rows[None], "ctx", split_axis=1, concat_axis=2, tiled=True),
        lax.all_to_all(featured_rows, "ctx", split_axis=1, concat_axis=2, tiled=True),
        lax.all_to_all(out_grad[None], "ctx", split_axis=1, concat_axis=2, tiled=True),
    )
    x_chan = x_chan[0]
    x_padded = jnp.pad(x_chan, ((0, 0), (6, 0)))
    grad_chan = grad_chan[0]
    tables = make_tables(blocks_a, tok_dev)
    key_full = featured[1].astype(jnp.float32)
    mixed_kv = key_full * featured[2].astype(jnp.float32)
    real_h, imag_h = forward_spectrum(filters[0].astype(jnp.float32), tables)
    real_w, imag_w = forward_spectrum(mixed_kv, tables)
    convolved = inverse_signal(
        real_h * real_w - imag_h * imag_w, real_h * imag_w + imag_h * real_w, tables
    )
    block_ch = 2
    block_count = channels // block_ch
    last_section = section_count - 1
    turns = block_count + section_count - 1
    dx_init = jnp.zeros((channels, length), jnp.bfloat16)

    def advance(turn_idx, carried):
        incoming, dz_all, dx_store, tap_acc = carried
        block_id = turn_idx - (last_section - section_idx)
        active = (block_id >= 0) & (block_id < block_count)
        first_ch = jnp.clip(block_id, 0, block_count - 1) * block_ch
        from_next = take_rows(grad_chan, first_ch, block_ch, 0)
        grad_in = jnp.where(section_idx == last_section, from_next, incoming).astype(jnp.float32)
        feat_blk = take_rows(featured, first_ch, block_ch, 1).astype(jnp.float32)
        grad_z = grad_in * feat_blk[0]
        grad_q = grad_in * take_rows(convolved, first_ch, block_ch, 0)
        real_d, imag_d = forward_spectrum(grad_z, tables)
        real_c, imag_c = times_conj(
            take_rows(real_h, first_ch, block_ch, 0),
            take_rows(imag_h, first_ch, block_ch, 0),
            real_d,
            imag_d,
        )
        grad_w = inverse_signal(real_c, imag_c, tables)
        grad_all = jnp.stack([grad_q, grad_w * feat_blk[2], grad_w * feat_blk[1]])
        in_blk = transposed(grad_all, take_rows(own_taps, first_ch, block_ch, 2)).astype(
            jnp.bfloat16
        )
        tap_new = tap_grads(take_rows(x_padded, first_ch, block_ch, 0), grad_all)
        tap_acc = masked_write(tap_acc, tap_new, first_ch, active, 2)
        dz_all = masked_write(dz_all, grad_z, first_ch, active, 0)
        outgoing = shifted(in_blk, "section", -1)
        dx_store = masked_write(dx_store, in_blk, first_ch, active, 0)
        return (outgoing, dz_all, dx_store, tap_acc)

    start_state = (
        jnp.zeros((block_ch, length), jnp.bfloat16),
        jnp.zeros((channels, length), jnp.float32),
        dx_init,
        jnp.zeros((3, 7, channels), jnp.float32),
    )
    final_state = lax.fori_loop(0, turns, advance, start_state)
    dz_all = final_state[1]
    dx_store = final_state[2]
    tap_acc = final_state[3]
    real_d, imag_d = forward_spectrum(dz_all, tables)
    real_c, imag_c = times_conj(real_w, imag_w, real_d, imag_d)
    filter_grad = inverse_signal(real_c, imag_c, tables)
    in_rows = lax.all_to_all(dx_store, "ctx", split_axis=1, concat_axis=0, tiled=True)
    return (in_rows[None], filter_grad[None], tap_acc[None])


TAPS = 7
GROUP = 16
MESH = pl.DeviceIdType.MESH
F32 = jnp.float32
BF16 = jnp.bfloat16


def right_angle_tables(blocks_a, block_b):
    total_n = blocks_a * block_b
    first_k = np.arange(blocks_a)
    phase_one = 2 * np.pi * np.outer(first_k + 0.25, np.arange(blocks_a)) / blocks_a
    one = np.stack([np.cos(phase_one), -np.sin(phase_one)])
    first = np.einsum("rka,cd->rkcad", one, np.eye(GROUP))
    first = first.reshape(2 * blocks_a * GROUP, blocks_a * GROUP)
    points = first_k[:, None, None] + 0.25 + blocks_a * np.arange(block_b)[None, None, :]
    phase_two = 2 * np.pi * np.arange(block_b)[None, :, None] * points / total_n
    real, imag = np.cos(phase_two), -np.sin(phase_two)
    second = np.concatenate(
        [np.concatenate([real, imag], axis=2), np.concatenate([-imag, real], axis=2)], axis=1
    )
    return tuple(
        array.astype(ml_dtypes.bfloat16)
        for array in (first, first.T / total_n, second, second.transpose(0, 2, 1))
    )


def mixer_kernel(
    sections,
    x_ref,
    og_ref,
    filt_ref,
    tap_ref,
    one_ref,
    one_inv_ref,
    two_ref,
    two_inv_ref,
    ig_out,
    fg_out,
    tg_out,
    xbuf,
    ogbuf,
    hbuf,
    tbuf,
    one_v,
    one_inv_v,
    two_v,
    two_inv_v,
    tapb,
    xs_ref,
    feat,
    sig,
    ybuf,
    spec,
    dspec,
    qbuf,
    cbuf,
    gwbuf,
    gbuf,
    igbuf,
    fgbuf,
    tgbuf,
    x_send,
    x_recv,
    og_send,
    og_recv,
    h_send,
    h_recv,
    t_send,
    t_recv,
    ig_send,
    ig_recv,
    fg_send,
    fg_recv,
    tg_send,
    tg_recv,
    table_sem,
):
    sec = lax.axis_index("section")
    ctx = lax.axis_index("ctx")
    blocks = xbuf.shape[1]
    rows = xbuf.shape[2]
    lanes = xbuf.shape[3]
    groups = rows // GROUP
    other = 1 - sec

    tables = [
        pltpu.make_async_copy(src, dst, table_sem.at[n])
        for n, (src, dst) in enumerate(
            ((one_ref, one_v), (two_ref, two_v), (one_inv_ref, one_inv_v), (two_inv_ref, two_inv_v))
        )
    ]

    barrier = pltpu.get_barrier_semaphore()

    def greet(step, carry):
        to_ctx = lax.rem(ctx + step, blocks)
        pl.semaphore_signal(barrier, inc=1, device_id=(other, to_ctx), device_id_type=MESH)

        @pl.when(step > 0)
        def _():
            pl.semaphore_signal(barrier, inc=1, device_id=(sec, to_ctx), device_id_type=MESH)

        return carry

    lax.fori_loop(0, blocks, greet, 0)
    for table in tables:
        table.start()
    pl.semaphore_wait(barrier, sections * blocks - 1)

    def row_block(to_sec, to_ctx):
        return pl.ds(pl.multiple_of((to_ctx * sections + to_sec) * rows, rows), rows)

    def half(which):
        return pl.ds(pl.multiple_of(which * rows, rows), rows)

    def remote(src, dst, send_sem, recv_sem, to_sec, to_ctx):
        pltpu.make_async_remote_copy(
            src_ref=src,
            dst_ref=dst,
            send_sem=send_sem,
            recv_sem=recv_sem,
            device_id=(to_sec, to_ctx),
            device_id_type=MESH,
        ).start()

    def await_bytes(ref, sem):
        pltpu.make_async_copy(ref, ref, sem).wait()

    remote(filt_ref.at[half(other)], hbuf.at[sec], h_send, h_recv, other, ctx)
    pltpu.make_async_copy(filt_ref.at[half(sec)], hbuf.at[sec], h_recv).start()
    remote(tap_ref.at[half(other)], tbuf.at[sec], t_send, t_recv, other, ctx)
    pltpu.make_async_copy(tap_ref.at[half(sec)], tbuf.at[sec], t_recv).start()

    def send_x(step, carry):
        to_ctx = lax.rem(ctx + step, blocks)
        dst = xbuf.at[sec, ctx]
        remote(x_ref.at[row_block(other, to_ctx)], dst, x_send, x_recv.at[sec], other, to_ctx)

        @pl.when(step > 0)
        def _():
            remote(x_ref.at[row_block(sec, to_ctx)], dst, x_send, x_recv.at[sec], sec, to_ctx)

        return carry

    pltpu.make_async_copy(
        x_ref.at[row_block(sec, ctx)], xbuf.at[sec, ctx], x_recv.at[sec]
    ).start()
    lax.fori_loop(0, blocks, send_x, 0)

    def send_og(step, carry):
        to_ctx = lax.rem(ctx + step, blocks)
        remote(og_ref.at[row_block(sec, to_ctx)], ogbuf.at[ctx], og_send, og_recv, sec, to_ctx)
        return carry

    pltpu.make_async_copy(og_ref.at[row_block(sec, ctx)], ogbuf.at[ctx], og_recv).start()
    lax.fori_loop(1, blocks, send_og, 0)

    def stage_one(blocks_of, first_row):
        cols = jnp.concatenate(
            [blocks_of(g).reshape(blocks * GROUP, lanes) for g in range(groups)], axis=1
        )
        out = jnp.dot(one_v[...], cols, preferred_element_type=F32).astype(BF16)
        out = out.reshape(2, blocks, GROUP, groups * lanes)
        for g in range(groups):
            for part in range(2):
                ybuf[:, pl.ds(first_row + g * GROUP, GROUP), pl.ds(part * lanes, lanes)] = out[
                    part, :, :, g * lanes : (g + 1) * lanes
                ]

    def stage_two(first_row, count, dst):
        def body(k, carry):
            dst[k, pl.ds(first_row, count)] = jnp.dot(
                ybuf[k, pl.ds(first_row, count)], two_v[k], preferred_element_type=F32
            )
            return carry

        lax.fori_loop(0, blocks, body, 0, unroll=4)

    def product(left, right, conj):
        left_r, left_i = left[:, :lanes], left[:, lanes:]
        right_r, right_i = right[:, :lanes], right[:, lanes:]
        if conj:
            real = left_r * right_r + left_i * right_i
            imag = left_r * right_i - left_i * right_r
        else:
            real = left_r * right_r - left_i * right_i
            imag = left_r * right_i + left_i * right_r
        return jnp.concatenate([real, imag], axis=1).astype(BF16)

    def inverse_two(operand, slots):
        def body(k, carry):
            out = jnp.dot(operand(k), two_inv_v[k], preferred_element_type=F32).astype(BF16)
            for slot in range(slots):
                for g in range(groups):
                    first = (slot * groups + g) * GROUP
                    for part in range(2):
                        qbuf[slot, part, k, :, pl.ds(g * lanes, lanes)] = out[
                            first : first + GROUP, part * lanes : (part + 1) * lanes
                        ]
            return carry

        lax.fori_loop(0, blocks, body, 0, unroll=4)

    def inverse_one(slot):
        out = jnp.dot(
            one_inv_v[...],
            qbuf[slot].reshape(2 * blocks * GROUP, groups * lanes),
            preferred_element_type=F32,
        )
        return out.reshape(blocks, GROUP, groups * lanes)

    tables[0].wait()
    tables[1].wait()
    await_bytes(hbuf, h_recv)
    for layer in range(sections):
        stage_one(
            lambda g: jnp.stack(
                [
                    hbuf[layer, pl.ds(g * GROUP, GROUP), pl.ds(a * lanes, lanes)]
                    for a in range(blocks)
                ]
            ),
            layer * rows,
        )
    stage_two(0, sections * rows, spec)

    await_bytes(tbuf, t_recv)
    for layer in range(sections):
        values = tbuf[layer]
        for n in range(3 * TAPS):
            tapb[layer, n] = jnp.broadcast_to(values[:, n : n + 1], (rows, lanes))

    lane = lax.broadcasted_iota(jnp.int32, (rows, lanes), 1)

    def features_of(layer):
        def body(a, before):
            window = xbuf[layer, a].astype(F32)
            sums = [None] * 3
            rolled = []
            for j in range(TAPS):
                if j == 0:
                    moved = window
                else:
                    turned = pltpu.roll(window, j, 1)
                    rolled.append(turned)
                    moved = jnp.where(lane < j, before[j - 1], turned)
                xs_ref[layer, j, a] = moved
                for i in range(3):
                    term = tapb[layer, i * TAPS + j] * moved
                    sums[i] = term if sums[i] is None else sums[i] + term
            rounded = [total.astype(BF16) for total in sums]
            for i in range(3):
                feat[layer, i, a] = rounded[i]
            sig[a] = (rounded[1].astype(F32) * rounded[2].astype(F32)).astype(BF16)
            return tuple(rolled)

        zero = jnp.zeros((rows, lanes), F32)
        lax.fori_loop(0, blocks, body, (zero,) * (TAPS - 1))

    mixed_row = sections * rows
    for layer in range(sections - 1, -1, -1):
        await_bytes(xbuf.at[layer], x_recv.at[layer])
        features_of(layer)
        stage_one(lambda g: sig[:, pl.ds(g * GROUP, GROUP), :], mixed_row + layer * rows)
    stage_two(mixed_row, sections * rows, spec)
    tables[2].wait()
    tables[3].wait()
    inverse_two(
        lambda k: product(
            spec[k, pl.ds(0, sections * rows)], spec[k, pl.ds(mixed_row, sections * rows)], False
        ),
        sections,
    )
    for layer in range(sections):
        out = inverse_one(layer)
        for g in range(groups):
            cbuf[layer, :, pl.ds(g * GROUP, GROUP), :] = out[:, :, g * lanes : (g + 1) * lanes]

    for layer in range(sections - 1, -1, -1):
        if layer == sections - 1:
            await_bytes(ogbuf, og_recv)
            carried = ogbuf
        else:
            carried = igbuf.at[layer + 1]

        sig[...] = (carried[...].astype(F32) * feat[layer, 0].astype(F32)).astype(BF16)
        stage_one(lambda g: sig[:, pl.ds(g * GROUP, GROUP), :], 0)
        stage_two(0, rows, dspec)

        def both(k):
            d_spec = dspec[k]
            with_h = product(spec[k, pl.ds(layer * rows, rows)], d_spec, True)
            with_w = product(spec[k, pl.ds(mixed_row + layer * rows, rows)], d_spec, True)
            return jnp.concatenate([with_h, with_w], axis=0)

        inverse_two(both, 2)
        out = inverse_one(0)
        for g in range(groups):
            gwbuf[:, pl.ds(g * GROUP, GROUP), :] = out[:, :, g * lanes : (g + 1) * lanes]

        def transposed_at(step, after):
            a = blocks - 1 - step
            grad_w = gwbuf[a]
            grads = (
                carried[a].astype(F32) * cbuf[layer, a],
                grad_w * feat[layer, 2, a].astype(F32),
                grad_w * feat[layer, 1, a].astype(F32),
            )
            for i in range(3):
                gbuf[i, a] = grads[i]
            total = None
            rolled = []
            for j in range(TAPS):
                part = tapb[layer, j] * grads[0]
                for i in range(1, 3):
                    part = part + tapb[layer, i * TAPS + j] * grads[i]
                if j == 0:
                    total = part
                else:
                    turned = pltpu.roll(part, lanes - j, 1)
                    rolled.append(turned)
                    total = total + jnp.where(lane < lanes - j, turned, after[j - 1])
            igbuf[layer, a] = total.astype(BF16)
            return tuple(rolled)

        zero = jnp.zeros((rows, lanes), F32)
        lax.fori_loop(0, blocks, transposed_at, (zero,) * (TAPS - 1))

        def send_ig(step, carry):
            to_ctx = lax.rem(ctx + step, blocks)
            src = igbuf.at[layer, to_ctx]
            dst = ig_out.at[row_block(sec, ctx)]
            local = (sec == layer) & (step == 0)

            @pl.when(local)
            def _():
                pltpu.make_async_copy(src, dst, ig_recv).start()

            @pl.when(jnp.logical_not(local))
            def _():
                remote(src, dst, ig_send, ig_recv, layer, to_ctx)

            return carry

        lax.fori_loop(0, blocks, send_ig, 0)

        out = inverse_one(1)
        for a in range(blocks):
            for g in range(groups):
                fgbuf[layer, pl.ds(g * GROUP, GROUP), pl.ds(a * lanes, lanes)] = out[
                    a, :, g * lanes : (g + 1) * lanes
                ]

        def send_home(src, dst, send_sem, recv_sem):
            @pl.when(sec == layer)
            def _():
                pltpu.make_async_copy(src, dst, recv_sem).start()

            @pl.when(sec != layer)
            def _():
                remote(src, dst, send_sem, recv_sem, layer, ctx)

        send_home(fgbuf.at[layer], fg_out.at[half(sec)], fg_send, fg_recv)

        for first in range(0, rows, 8):
            def add_taps(a, sums):
                grads = [gbuf[i, a, pl.ds(first, 8)] for i in range(3)]
                new = []
                for j in range(TAPS):
                    moved = xs_ref[layer, j, a, pl.ds(first, 8)]
                    for i in range(3):
                        new.append(sums[j * 3 + i] + grads[i] * moved)
                return tuple(new)

            zero_8 = jnp.zeros((8, lanes), F32)
            sums = lax.fori_loop(0, blocks, add_taps, (zero_8,) * (3 * TAPS))
            lane_8 = lax.broadcasted_iota(jnp.int32, (8, lanes), 1)
            packed = zero_8
            for j in range(TAPS):
                for i in range(3):
                    column = jnp.sum(sums[j * 3 + i], axis=1, keepdims=True)
                    packed = jnp.where(lane_8 == i * TAPS + j, column, packed)
            tgbuf[layer, pl.ds(first, 8)] = packed
        send_home(tgbuf.at[layer], tg_out.at[half(sec)], tg_send, tg_recv)

    others = sections * blocks - 1
    await_bytes(x_ref.at[pl.ds(0, others * rows)], x_send)
    await_bytes(og_ref.at[pl.ds(0, (blocks - 1) * rows)], og_send)
    await_bytes(filt_ref.at[pl.ds(0, rows)], h_send)
    await_bytes(tap_ref.at[pl.ds(0, rows)], t_send)
    await_bytes(ig_out.at[pl.ds(0, others * rows)], ig_send)
    await_bytes(fg_out.at[pl.ds(0, rows)], fg_send)
    await_bytes(tg_out.at[pl.ds(0, rows)], tg_send)
    await_bytes(ig_out, ig_recv)
    await_bytes(fg_out, fg_recv)
    await_bytes(tg_out, tg_recv)


def kernel_shards(inputs, out_grad, filters, conv_taps):
    sections = lax.axis_size("section")
    blocks = lax.axis_size("ctx")
    ctx_idx = lax.axis_index("ctx")
    _, depth, lanes = inputs.shape
    _, channels, length = filters.shape
    rows = channels // sections
    tables = right_angle_tables(blocks, lanes)
    own = lax.dynamic_slice_in_dim(conv_taps[0], ctx_idx * channels, channels, 2)
    own = own.reshape(3 * TAPS, channels).T
    own = jnp.pad(own, ((0, 0), (0, lanes - 3 * TAPS)))
    vmem = pltpu.VMEM
    dma = pltpu.SemaphoreType.DMA
    any_spec = pl.BlockSpec(memory_space=pl.ANY)
    spectrum_rows = 2 * sections * rows
    in_grad, filter_grad, tap_sums = pl.pallas_call(
        functools.partial(mixer_kernel, sections),
        out_shape=(
            jax.ShapeDtypeStruct((depth, lanes), BF16),
            jax.ShapeDtypeStruct((channels, length), F32),
            jax.ShapeDtypeStruct((channels, lanes), F32),
        ),
        in_specs=[any_spec] * 8,
        out_specs=(any_spec,) * 3,
        scratch_shapes=[
            vmem((sections, blocks, rows, lanes), BF16),
            vmem((blocks, rows, lanes), BF16),
            vmem((sections, rows, length), BF16),
            vmem((sections, rows, lanes), F32),
            vmem(tables[0].shape, BF16),
            vmem(tables[1].shape, BF16),
            vmem(tables[2].shape, BF16),
            vmem(tables[3].shape, BF16),
            vmem((sections, 3 * TAPS, rows, lanes), F32),
            vmem((sections, TAPS, blocks, rows, lanes), F32),
            vmem((sections, 3, blocks, rows, lanes), BF16),
            vmem((blocks, rows, lanes), BF16),
            vmem((blocks, spectrum_rows, 2 * lanes), BF16),
            vmem((blocks, spectrum_rows, 2 * lanes), F32),
            vmem((blocks, rows, 2 * lanes), F32),
            vmem((2, 2, blocks, GROUP, rows // GROUP * lanes), BF16),
            vmem((sections, blocks, rows, lanes), F32),
            vmem((blocks, rows, lanes), F32),
            vmem((3, blocks, rows, lanes), F32),
            vmem((sections, blocks, rows, lanes), BF16),
            vmem((sections, rows, length), F32),
            vmem((sections, rows, lanes), F32),
            dma(()),
            dma((sections,)),
            dma(()),
            dma(()),
            dma(()),
            dma(()),
            dma(()),
            dma(()),
            dma(()),
            dma(()),
            dma(()),
            dma(()),
            dma(()),
            dma(()),
            dma((4,)),
        ],
        compiler_params=pltpu.CompilerParams(
            collective_id=0, has_side_effects=True, vmem_limit_bytes=40 * 2**20
        ),
    )(inputs[0], out_grad, filters[0], own, *(jnp.asarray(table) for table in tables))
    tap_grad = tap_sums[:, : 3 * TAPS].T.reshape(3, TAPS, channels)
    return (in_grad[None], filter_grad[None], tap_grad[None])


def solution(mesh):
    placed = (
        P("section", None, "ctx"),
        P(None, "ctx"),
        P("section", "ctx", None),
        P("section", None, None, None),
    )

    def run(inputs, out_grad, filters, conv_taps):
        sections, blocks = mesh.shape["section"], mesh.shape["ctx"]
        rows = filters.shape[1] // (sections * blocks)
        lanes = inputs.shape[2] // blocks
        fits = sections == 2 and rows % GROUP == 0 and lanes == 128
        return jax.shard_map(
            kernel_shards if fits else shards,
            mesh=mesh,
            in_specs=placed,
            out_specs=(
                P("section", None, "ctx"),
                P("section", "ctx", None),
                P("section", None, None, "ctx"),
            ),
            check_vma=False,
        )(inputs, out_grad, filters, conv_taps)

    return run
```

profile of v0, /device:TPU:0, one launch (start us, length us, event | category | flops | bytes accessed | tf_op | source)
XLA Modules:
  0.0 52.6 jit_solution(3733037980499952775)
XLA Ops:
  0.6 0.0 copy-start
  0.6 0.9 %copy-done = f32[1,3,7,1024]{3,0,2,1:T(1,128)S(1)} copy-done((f32[1,3,7,1024]{3,0,2,1:T(1,128)S(1)}, f32[1,3,7,1024]{3,0,2,1:T(1,128)}, u32[]{:S(2)}) %copy-start) | copy-done | bytes 86040
  1.5 0.1 dynamic-slice_reduce_fusion
  1.6 0.1 copy.13
  1.7 0.0 copy-start.1
  1.8 1.6 %copy-done.1 = bf16[16,256,256]{2,1,0:T(8,128)(2,1)S(1)} copy-done((bf16[16,256,256]{2,1,0:T(8,128)(2,1)S(1)}, bf16[16,256,256]{2,1,0:T(8,128)(2,1)}, u32[]{:S(2)}) %copy-start.1) | copy-done | bytes 2097176
  3.3 0.0 copy-start.2
  3.3 1.6 %copy-done.2 = bf16[16,256,256]{2,1,0:T(8,128)(2,1)S(1)} copy-done((bf16[16,256,256]{2,1,0:T(8,128)(2,1)S(1)}, bf16[16,256,256]{2,1,0:T(8,128)(2,1)}, u32[]{:S(2)}) %copy-start.2) | copy-done | bytes 2097176
  4.9 0.0 copy-start.3
  4.9 0.9 %copy-done.3 = bf16[1,1024,128]{2,1,0:T(8,128)(2,1)S(1)} copy-done((bf16[1,1024,128]{2,1,0:T(8,128)(2,1)S(1)}, bf16[1,1024,128]{2,1,0:T(8,128)(2,1)}, u32[]{:S(2)}) %copy-start.3) | copy-done | bytes 262168
  5.9 0.0 copy-start.4
  5.9 0.9 %copy-done.4 = bf16[1024,128]{1,0:T(8,128)(2,1)S(1)} copy-done((bf16[1024,128]{1,0:T(8,128)(2,1)S(1)}, bf16[1024,128]{1,0:T(8,128)(2,1)}, u32[]{:S(2)}) %copy-start.4) | copy-done | bytes 262168
  6.8 0.0 copy-start.5
  6.8 0.9 %copy-done.5 = bf16[1,64,2048]{2,1,0:T(8,128)(2,1)S(1)} copy-done((bf16[1,64,2048]{2,1,0:T(8,128)(2,1)S(1)}, bf16[1,64,2048]{2,1,0:T(8,128)(2,1)}, u32[]{:S(2)}) %copy-start.5) | copy-done | bytes 262168
  7.8 0.0 copy-start.6
  7.8 0.9 %copy-done.6 = bf16[256,512]{1,0:T(8,128)(2,1)S(1)} copy-done((bf16[256,512]{1,0:T(8,128)(2,1)S(1)}, bf16[256,512]{1,0:T(8,128)(2,1)}, u32[]{:S(2)}) %copy-start.6) | copy-done | bytes 262168
  8.7 0.0 copy-start.7
  8.7 0.9 %copy-done.7 = bf16[512,256]{1,0:T(8,128)(2,1)S(1)} copy-done((bf16[512,256]{1,0:T(8,128)(2,1)S(1)}, bf16[512,256]{1,0:T(8,128)(2,1)}, u32[]{:S(2)}) %copy-start.7) | copy-done | bytes 262168
  9.7 40.7 %shard_map.103 = (bf16[1024,128]{1,0:T(8,128)(2,1)S(1)}, f32[64,2048]{1,0:T(8,128)S(1)}, f32[64,128]{1,0:T(8,128)S(1)}) custom-call(bf16[1024,128]{1,0:T(8,128)(2,1)S(1)} %bitcast.9, bf16[1024,128]{1,0:T(8,128)(2,1)S(1)} %copy-done.4, bf16[64,2048]{1,0:T(8,128)(2,1)S(1)} %bitcast.10, f32[64,128]{1,0:T(8,128)S(1)} %pad.4.tap_ref, ...), custom_call_target="tpu_custom_call" | custom-call | tf_op jit(solution)/shard_map/pallas_call | solution.py:621
  50.4 0.1 copy.14
  50.5 0.6 %broadcast_in_dim_reshape.4 = f32[1,3,7,64]{3,0,2,1:T(1,128)} reshape(f32[21,64]{1,0:T(8,128)S(1)} %copy.14) | data formatting | bytes 10752 | tf_op jit(solution)/shard_map/broadcast_in_dim;reshape | solution.py:674
  51.1 0.7 %copy.19 = bf16[1,1024,128]{2,1,0:T(8,128)(2,1)} copy(bf16[1,1024,128]{2,1,0:T(8,128)(2,1)S(1)} %bitcast.8) | data formatting | bytes 524288
  51.8 0.8 %copy.20 = f32[1,64,2048]{2,1,0:T(8,128)} copy(f32[1,64,2048]{2,1,0:T(8,128)S(1)} %bitcast.7) | data formatting | bytes 1048576
  (3 shorter events, 0.0 us)
Async XLA Ops:
  0.6 0.9 %copy-start = (f32[1,3,7,1024]{3,0,2,1:T(1,128)S(1)}, f32[1,3,7,1024]{3,0,2,1:T(1,128)}, u32[]{:S(2)}) copy-start(f32[1,3,7,1024]{3,0,2,1:T(1,128)} %param.11) | copy-start | bytes 258052
  1.7 1.6 %copy-start.1 = (bf16[16,256,256]{2,1,0:T(8,128)(2,1)S(1)}, bf16[16,256,256]{2,1,0:T(8,128)(2,1)}, u32[]{:S(2)}) copy-start(bf16[16,256,256]{2,1,0:T(8,128)(2,1)} %constant.24.clone.two_inv_ref) | copy-start | bytes 6291460
  3.3 1.6 %copy-start.2 = (bf16[16,256,256]{2,1,0:T(8,128)(2,1)S(1)}, bf16[16,256,256]{2,1,0:T(8,128)(2,1)}, u32[]{:S(2)}) copy-start(bf16[16,256,256]{2,1,0:T(8,128)(2,1)} %constant.23.clone.two_ref) | copy-start | bytes 6291460
  4.9 0.9 %copy-start.3 = (bf16[1,1024,128]{2,1,0:T(8,128)(2,1)S(1)}, bf16[1,1024,128]{2,1,0:T(8,128)(2,1)}, u32[]{:S(2)}) copy-start(bf16[1,1024,128]{2,1,0:T(8,128)(2,1)} %param.8) | copy-start | bytes 786436
  5.9 0.9 %copy-start.4 = (bf16[1024,128]{1,0:T(8,128)(2,1)S(1)}, bf16[1024,128]{1,0:T(8,128)(2,1)}, u32[]{:S(2)}) copy-start(bf16[1024,128]{1,0:T(8,128)(2,1)} %og_ref.1) | copy-start | bytes 786436
  6.8 0.9 %copy-start.5 = (bf16[1,64,2048]{2,1,0:T(8,128)(2,1)S(1)}, bf16[1,64,2048]{2,1,0:T(8,128)(2,1)}, u32[]{:S(2)}) copy-start(bf16[1,64,2048]{2,1,0:T(8,128)(2,1)} %param.10) | copy-start | bytes 786436
  7.8 0.9 %copy-start.6 = (bf16[256,512]{1,0:T(8,128)(2,1)S(1)}, bf16[256,512]{1,0:T(8,128)(2,1)}, u32[]{:S(2)}) copy-start(bf16[256,512]{1,0:T(8,128)(2,1)} %constant.22.clone.one_inv_ref) | copy-start | bytes 786436
  8.7 0.9 %copy-start.7 = (bf16[512,256]{1,0:T(8,128)(2,1)S(1)}, bf16[512,256]{1,0:T(8,128)(2,1)}, u32[]{:S(2)}) copy-start(bf16[512,256]{1,0:T(8,128)(2,1)} %constant.21.clone.one_ref) | copy-start | bytes 786436
where the time goes:
time: 53 us; the launch traced here: 52.6 us
  Pallas kernels  40.7 us (77%)
  local copies, waits for them, and re-layouts  11.2 us (21%)
  between operations  0.69 us (1%)
    pallas_call x1, Pallas kernels, kernel_shards(): pl.pallas_call(functools.partial(mixer_kernel, sections), out_shape=(jax....  40.7 us
    unnamed x18, local copies, waits for them, and re-layouts  10.3 us

commit v1 on v0

--- a/solution.py
+++ b/solution.py
@@ -247,6 +247,8 @@
     xbuf,
     ogbuf,
     hbuf,
+    tap_blk,
+    tap_rows,
     tbuf,
     one_v,
     one_inv_v,
@@ -258,7 +260,6 @@
     sig,
     ybuf,
     spec,
-    dspec,
     qbuf,
     cbuf,
     gwbuf,
@@ -266,6 +267,7 @@
     igbuf,
     fgbuf,
     tgbuf,
+    tgin,
     x_send,
     x_recv,
     og_send,
@@ -281,6 +283,7 @@
     tg_send,
     tg_recv,
     table_sem,
+    blk_sem,
 ):
     sec = lax.axis_index("section")
     ctx = lax.axis_index("ctx")
@@ -296,6 +299,12 @@
             ((one_ref, one_v), (two_ref, two_v), (one_inv_ref, one_inv_v), (two_inv_ref, two_inv_v))
         )
     ]
+
+    channels = sections * rows
+    tap_first = ctx * channels
+    tap_lane = pl.multiple_of(tap_first // lanes * lanes, lanes)
+    tap_load = pltpu.make_async_copy(tap_ref.at[:, :, pl.ds(tap_lane, lanes)], tap_blk, blk_sem)
+    tap_load.start()
 
     barrier = pltpu.get_barrier_semaphore()
 
@@ -335,24 +344,21 @@
 
     remote(filt_ref.at[half(other)], hbuf.at[sec], h_send, h_recv, other, ctx)
     pltpu.make_async_copy(filt_ref.at[half(sec)], hbuf.at[sec], h_recv).start()
-    remote(tap_ref.at[half(other)], tbuf.at[sec], t_send, t_recv, other, ctx)
-    pltpu.make_async_copy(tap_ref.at[half(sec)], tbuf.at[sec], t_recv).start()
-
-    def send_x(step, carry):
-        to_ctx = lax.rem(ctx + step, blocks)
-        dst = xbuf.at[sec, ctx]
-        remote(x_ref.at[row_block(other, to_ctx)], dst, x_send, x_recv.at[sec], other, to_ctx)
-
-        @pl.when(step > 0)
-        def _():
-            remote(x_ref.at[row_block(sec, to_ctx)], dst, x_send, x_recv.at[sec], sec, to_ctx)
-
-        return carry
+
+    def send_x(to_sec):
+        def send(step, carry):
+            to_ctx = lax.rem(ctx + step, blocks)
+            src = x_ref.at[row_block(to_sec, to_ctx)]
+            remote(src, xbuf.at[sec, ctx], x_send, x_recv.at[sec], to_sec, to_ctx)
+            return carry
+
+        return send
 
     pltpu.make_async_copy(
         x_ref.at[row_block(sec, ctx)], xbuf.at[sec, ctx], x_recv.at[sec]
     ).start()
-    lax.fori_loop(0, blocks, send_x, 0)
+    lax.fori_loop(1, blocks, send_x(sec), 0)
+    lax.fori_loop(0, blocks, send_x(other), 0)
 
     def send_og(step, carry):
         to_ctx = lax.rem(ctx + step, blocks)
@@ -361,6 +367,18 @@
 
     pltpu.make_async_copy(og_ref.at[row_block(sec, ctx)], ogbuf.at[ctx], og_recv).start()
     lax.fori_loop(1, blocks, send_og, 0)
+
+    tap_load.wait()
+    tap_rows[...] = jnp.zeros_like(tap_rows)
+    tap_rows[pl.ds(0, 3 * TAPS)] = tap_blk[...].reshape(3 * TAPS, lanes)
+    tap_rows[...] = tap_rows[...].T
+
+    def tap_half(which):
+        first = lax.rem(tap_first, lanes) + which * rows
+        return tap_rows.at[pl.ds(pl.multiple_of(first, rows), rows)]
+
+    remote(tap_half(other), tbuf.at[sec], t_send, t_recv, other, ctx)
+    pltpu.make_async_copy(tap_half(sec), tbuf.at[sec], t_recv).start()
 
     def stage_one(blocks_of, first_row):
         cols = jnp.concatenate(
@@ -374,14 +392,15 @@
                     part, :, :, g * lanes : (g + 1) * lanes
                 ]
 
-    def stage_two(first_row, count, dst):
-        def body(k, carry):
-            dst[k, pl.ds(first_row, count)] = jnp.dot(
-                ybuf[k, pl.ds(first_row, count)], two_v[k], preferred_element_type=F32
-            )
+    def stage_two(k, first_row, count):
+        return jnp.dot(ybuf[k, pl.ds(first_row, count)], two_v[k], preferred_element_type=F32)
+
+    def each_point(body):
+        def step(k, carry):
+            body(k)
             return carry
 
-        lax.fori_loop(0, blocks, body, 0, unroll=4)
+        lax.fori_loop(0, blocks, step, 0, unroll=True)
 
     def product(left, right, conj):
         left_r, left_i = left[:, :lanes], left[:, lanes:]
@@ -394,19 +413,15 @@
             imag = left_r * right_i + left_i * right_r
         return jnp.concatenate([real, imag], axis=1).astype(BF16)
 
-    def inverse_two(operand, slots):
-        def body(k, carry):
-            out = jnp.dot(operand(k), two_inv_v[k], preferred_element_type=F32).astype(BF16)
-            for slot in range(slots):
-                for g in range(groups):
-                    first = (slot * groups + g) * GROUP
-                    for part in range(2):
-                        qbuf[slot, part, k, :, pl.ds(g * lanes, lanes)] = out[
-                            first : first + GROUP, part * lanes : (part + 1) * lanes
-                        ]
-            return carry
-
-        lax.fori_loop(0, blocks, body, 0, unroll=4)
+    def inverse_two(k, operand, slots):
+        out = jnp.dot(operand, two_inv_v[k], preferred_element_type=F32).astype(BF16)
+        for slot in range(slots):
+            for g in range(groups):
+                first = (slot * groups + g) * GROUP
+                for part in range(2):
+                    qbuf[slot, part, k, :, pl.ds(g * lanes, lanes)] = out[
+                        first : first + GROUP, part * lanes : (part + 1) * lanes
+                    ]
 
     def inverse_one(slot):
         out = jnp.dot(
@@ -429,7 +444,11 @@
             ),
             layer * rows,
         )
-    stage_two(0, sections * rows, spec)
+
+    def filter_point(k):
+        spec[k, pl.ds(0, channels)] = stage_two(k, 0, channels)
+
+    each_point(filter_point)
 
     await_bytes(tbuf, t_recv)
     for layer in range(sections):
@@ -462,26 +481,35 @@
             return tuple(rolled)
 
         zero = jnp.zeros((rows, lanes), F32)
-        lax.fori_loop(0, blocks, body, (zero,) * (TAPS - 1))
+        lax.fori_loop(0, blocks, body, (zero,) * (TAPS - 1), unroll=2)
 
     mixed_row = sections * rows
     for layer in range(sections - 1, -1, -1):
         await_bytes(xbuf.at[layer], x_recv.at[layer])
         features_of(layer)
         stage_one(lambda g: sig[:, pl.ds(g * GROUP, GROUP), :], mixed_row + layer * rows)
-    stage_two(mixed_row, sections * rows, spec)
     tables[2].wait()
     tables[3].wait()
-    inverse_two(
-        lambda k: product(
-            spec[k, pl.ds(0, sections * rows)], spec[k, pl.ds(mixed_row, sections * rows)], False
-        ),
-        sections,
-    )
+
+    def mixed_point(k):
+        mixed = stage_two(k, mixed_row, channels)
+        spec[k, pl.ds(mixed_row, channels)] = mixed
+        inverse_two(k, product(spec[k, pl.ds(0, channels)], mixed, False), sections)
+
+    each_point(mixed_point)
     for layer in range(sections):
         out = inverse_one(layer)
         for g in range(groups):
             cbuf[layer, :, pl.ds(g * GROUP, GROUP), :] = out[:, :, g * lanes : (g + 1) * lanes]
+
+    def send_home(layer, src, dst, send_sem, recv_sem):
+        @pl.when(sec == layer)
+        def _():
+            pltpu.make_async_copy(src, dst, recv_sem).start()
+
+        @pl.when(sec != layer)
+        def _():
+            remote(src, dst, send_sem, recv_sem, layer, ctx)
 
     for layer in range(sections - 1, -1, -1):
         if layer == sections - 1:
@@ -492,15 +520,14 @@
 
         sig[...] = (carried[...].astype(F32) * feat[layer, 0].astype(F32)).astype(BF16)
         stage_one(lambda g: sig[:, pl.ds(g * GROUP, GROUP), :], 0)
-        stage_two(0, rows, dspec)
-
-        def both(k):
-            d_spec = dspec[k]
+
+        def grad_point(k):
+            d_spec = stage_two(k, 0, rows)
             with_h = product(spec[k, pl.ds(layer * rows, rows)], d_spec, True)
             with_w = product(spec[k, pl.ds(mixed_row + layer * rows, rows)], d_spec, True)
-            return jnp.concatenate([with_h, with_w], axis=0)
-
-        inverse_two(both, 2)
+            inverse_two(k, jnp.concatenate([with_h, with_w], axis=0), 2)
+
+        each_point(grad_point)
         out = inverse_one(0)
         for g in range(groups):
             gwbuf[:, pl.ds(g * GROUP, GROUP), :] = out[:, :, g * lanes : (g + 1) * lanes]
@@ -514,7 +541,7 @@
                 grad_w * feat[layer, 1, a].astype(F32),
             )
             for i in range(3):
-                gbuf[i, a] = grads[i]
+                gbuf[layer, i, a] = grads[i]
             total = None
             rolled = []
             for j in range(TAPS):
@@ -531,7 +558,7 @@
             return tuple(rolled)
 
         zero = jnp.zeros((rows, lanes), F32)
-        lax.fori_loop(0, blocks, transposed_at, (zero,) * (TAPS - 1))
+        lax.fori_loop(0, blocks, transposed_at, (zero,) * (TAPS - 1), unroll=2)
 
         def send_ig(step, carry):
             to_ctx = lax.rem(ctx + step, blocks)
@@ -556,22 +583,14 @@
             for g in range(groups):
                 fgbuf[layer, pl.ds(g * GROUP, GROUP), pl.ds(a * lanes, lanes)] = out[
                     a, :, g * lanes : (g + 1) * lanes
-                ]
-
-        def send_home(src, dst, send_sem, recv_sem):
-            @pl.when(sec == layer)
-            def _():
-                pltpu.make_async_copy(src, dst, recv_sem).start()
-
-            @pl.when(sec != layer)
-            def _():
-                remote(src, dst, send_sem, recv_sem, layer, ctx)
-
-        send_home(fgbuf.at[layer], fg_out.at[half(sec)], fg_send, fg_recv)
-
+                ].astype(BF16)
+
+        send_home(layer, fgbuf.at[layer], fg_out.at[half(sec)], fg_send, fg_recv)
+
+    for layer in range(sections - 1, -1, -1):
         for first in range(0, rows, 8):
             def add_taps(a, sums):
-                grads = [gbuf[i, a, pl.ds(first, 8)] for i in range(3)]
+                grads = [gbuf[layer, i, a, pl.ds(first, 8)] for i in range(3)]
                 new = []
                 for j in range(TAPS):
                     moved = xs_ref[layer, j, a, pl.ds(first, 8)]
@@ -580,7 +599,7 @@
                 return tuple(new)
 
             zero_8 = jnp.zeros((8, lanes), F32)
-            sums = lax.fori_loop(0, blocks, add_taps, (zero_8,) * (3 * TAPS))
+            sums = lax.fori_loop(0, blocks, add_taps, (zero_8,) * (3 * TAPS), unroll=4)
             lane_8 = lax.broadcasted_iota(jnp.int32, (8, lanes), 1)
             packed = zero_8
             for j in range(TAPS):
@@ -588,49 +607,51 @@
                     column = jnp.sum(sums[j * 3 + i], axis=1, keepdims=True)
                     packed = jnp.where(lane_8 == i * TAPS + j, column, packed)
             tgbuf[layer, pl.ds(first, 8)] = packed
-        send_home(tgbuf.at[layer], tg_out.at[half(sec)], tg_send, tg_recv)
+        send_home(layer, tgbuf.at[layer], tgin.at[half(sec)], tg_send, tg_recv)
 
     others = sections * blocks - 1
     await_bytes(x_ref.at[pl.ds(0, others * rows)], x_send)
     await_bytes(og_ref.at[pl.ds(0, (blocks - 1) * rows)], og_send)
     await_bytes(filt_ref.at[pl.ds(0, rows)], h_send)
-    await_bytes(tap_ref.at[pl.ds(0, rows)], t_send)
+    await_bytes(tbuf.at[0], t_send)
     await_bytes(ig_out.at[pl.ds(0, others * rows)], ig_send)
     await_bytes(fg_out.at[pl.ds(0, rows)], fg_send)
-    await_bytes(tg_out.at[pl.ds(0, rows)], tg_send)
+    await_bytes(tgbuf.at[0], tg_send)
+    await_bytes(tgin, tg_recv)
+    tg_out[...] = tgin[...].T[: 3 * TAPS].reshape(3 * TAPS, 1, channels)
+    await_bytes(fg_out, fg_recv)
     await_bytes(ig_out, ig_recv)
-    await_bytes(fg_out, fg_recv)
-    await_bytes(tg_out, tg_recv)
 
 
 def kernel_shards(inputs, out_grad, filters, conv_taps):
     sections = lax.axis_size("section")
     blocks = lax.axis_size("ctx")
-    ctx_idx = lax.axis_index("ctx")
     _, depth, lanes = inputs.shape
     _, channels, length = filters.shape
     rows = channels // sections
     tables = right_angle_tables(blocks, lanes)
-    own = lax.dynamic_slice_in_dim(conv_taps[0], ctx_idx * channels, channels, 2)
-    own = own.reshape(3 * TAPS, channels).T
-    own = jnp.pad(own, ((0, 0), (0, lanes - 3 * TAPS)))
+    taps = conv_taps.reshape(3 * TAPS, 1, depth)
     vmem = pltpu.VMEM
     dma = pltpu.SemaphoreType.DMA
     any_spec = pl.BlockSpec(memory_space=pl.ANY)
+    hbm_spec = pl.BlockSpec(memory_space=pl.ANY)
+    vmem_spec = pl.BlockSpec(memory_space=pltpu.VMEM)
     spectrum_rows = 2 * sections * rows
     in_grad, filter_grad, tap_sums = pl.pallas_call(
         functools.partial(mixer_kernel, sections),
         out_shape=(
             jax.ShapeDtypeStruct((depth, lanes), BF16),
-            jax.ShapeDtypeStruct((channels, length), F32),
-            jax.ShapeDtypeStruct((channels, lanes), F32),
+            jax.ShapeDtypeStruct((channels, length), BF16),
+            jax.ShapeDtypeStruct((3 * TAPS, 1, channels), F32),
         ),
-        in_specs=[any_spec] * 8,
-        out_specs=(any_spec,) * 3,
+        in_specs=[hbm_spec] * 8,
+        out_specs=(any_spec, any_spec, vmem_spec),
         scratch_shapes=[
             vmem((sections, blocks, rows, lanes), BF16),
             vmem((blocks, rows, lanes), BF16),
             vmem((sections, rows, length), BF16),
+            vmem((3 * TAPS, 1, lanes), F32),
+            vmem((lanes, lanes), F32),
             vmem((sections, rows, lanes), F32),
             vmem(tables[0].shape, BF16),
             vmem(tables[1].shape, BF16),
@@ -642,14 +663,14 @@
             vmem((blocks, rows, lanes), BF16),
             vmem((blocks, spectrum_rows, 2 * lanes), BF16),
             vmem((blocks, spectrum_rows, 2 * lanes), F32),
-            vmem((blocks, rows, 2 * lanes), F32),
             vmem((2, 2, blocks, GROUP, rows // GROUP * lanes), BF16),
             vmem((sections, blocks, rows, lanes), F32),
             vmem((blocks, rows, lanes), F32),
-            vmem((3, blocks, rows, lanes), F32),
+            vmem((sections, 3, blocks, rows, lanes), F32),
             vmem((sections, blocks, rows, lanes), BF16),
-            vmem((sections, rows, length), F32),
+            vmem((sections, rows, length), BF16),
             vmem((sections, rows, lanes), F32),
+            vmem((channels, lanes), F32),
             dma(()),
             dma((sections,)),
             dma(()),
@@ -665,13 +686,14 @@
             dma(()),
             dma(()),
             dma((4,)),
+            dma(()),
         ],
         compiler_params=pltpu.CompilerParams(
-            collective_id=0, has_side_effects=True, vmem_limit_bytes=40 * 2**20
+            collective_id=0, has_side_effects=True, vmem_limit_bytes=58 * 2**20
         ),
-    )(inputs[0], out_grad, filters[0], own, *(jnp.asarray(table) for table in tables))
-    tap_grad = tap_sums[:, : 3 * TAPS].T.reshape(3, TAPS, channels)
-    return (in_grad[None], filter_grad[None], tap_grad[None])
+    )(inputs[0], out_grad, filters[0], taps, *(jnp.asarray(table) for table in tables))
+    tap_grad = tap_sums.reshape(1, 3, TAPS, channels)
+    return (in_grad[None], filter_grad.astype(F32)[None], tap_grad)
 
 
 def solution(mesh):
@@ -686,7 +708,7 @@
         sections, blocks = mesh.shape["section"], mesh.shape["ctx"]
         rows = filters.shape[1] // (sections * blocks)
         lanes = inputs.shape[2] // blocks
-        fits = sections == 2 and rows % GROUP == 0 and lanes == 128
+        fits = sections == 2 and rows % GROUP == 0 and lanes == 128 and lanes % (sections * rows) == 0
         return jax.shard_map(
             kernel_shards if fits else shards,
             mesh=mesh,

time: 53 us -> 39 us (0.74)
  local copies, waits for them, and re-layouts: 11.2 us -> 2.97 us
  Pallas kernels: 40.7 us -> 33.4 us
  other arithmetic: 0 us -> 1.78 us
    pallas_call x1, Pallas kernels: 40.7 us -> 33.4 us  [kernel_shards(): pl.pallas_call(functools.partial(mixer_kernel, sections), out_shape=(jax....]
    unnamed x18 -> x2, local copies, waits for them, and re-layouts: 10.3 us -> 2.97 us
    broadcast_in_dim x0 -> x1, other arithmetic: none -> 1.78 us  [kernel_shards(): return (in_grad[None], filter_grad.astype(F32)[None], tap_grad)]
    another operation x1 -> x0, local copies, waits for them, and re-layouts: 0.63 us -> none  [kernel_shards(): return (in_grad[None], filter_grad[None], tap_grad[None])]
where the time goes in v1:
time: 39 us; the launch traced here: 38.8 us
  Pallas kernels  33.4 us (86%)
  local copies, waits for them, and re-layouts  2.97 us (8%)
  other arithmetic  1.78 us (5%)
  between operations  0.64 us (2%)
    pallas_call x1, Pallas kernels, kernel_shards(): pl.pallas_call(functools.partial(mixer_kernel, sections), out_shape=(jax....  33.4 us
    unnamed x2, local copies, waits for them, and re-layouts  2.97 us
    broadcast_in_dim x1, other arithmetic, kernel_shards(): return (in_grad[None], filter_grad.astype(F32)[None], tap_grad)  1.78 us

profile of v1, /device:TPU:0, one launch (start us, length us, event | category | flops | bytes accessed | tf_op | source)
XLA Modules:
  0.0 38.8 jit_solution(1326890290710977274)
XLA Ops:
  0.6 33.4 %shard_map.103 = (bf16[1024,128]{1,0:T(8,128)(2,1)}, bf16[64,2048]{1,0:T(8,128)(2,1)}, f32[21,1,64]{2,1,0:T(1,128)}) custom-call(bf16[1024,128]{1,0:T(8,128)(2,1)} %bitcast.8, bf16[1024,128]{1,0:T(8,128)(2,1)} %og_ref.1, bf16[64,2048]{1,0:T(8,128)(2,1)} %bitcast.9, f32[21,1,1024]{2,1,0:T(1,128)} %bitcast.11, bf16[512,256]{1,0:T(8,128)(2,1)} %constant.8.clone.one_ref, ...), custom_call_target="tpu_custom_call" | custom-call | tf_op jit(solution)/shard_map/pallas_call | solution.py:640
  34.0 1.8 %bitcast_convert_fusion = f32[1,64,2048]{2,1,0:T(8,128)} fusion(bf16[64,2048]{1,0:T(8,128)(2,1)} %get-tuple-element.7), kind=kLoop, calls=%fused_computation | loop fusion | flops 131072 | bytes 786432 | tf_op jit(solution)/shard_map/broadcast_in_dim | solution.py:696
  35.8 1.7 %copy.13 = bf16[1,1024,128]{2,1,0:T(8,128)(2,1)} copy(bf16[1,1024,128]{2,1,0:T(8,128)(2,1)} %bitcast.10) | data formatting | bytes 524288
  37.5 1.3 %copy.14 = f32[1,3,7,64]{3,0,2,1:T(1,128)} copy(f32[1,3,7,64]{3,0,2,1:T(1,128)} %bitcast.12) | data formatting | bytes 10752

commit v2 on v1

--- a/solution.py
+++ b/solution.py
@@ -318,7 +318,7 @@
 
         return carry
 
-    lax.fori_loop(0, blocks, greet, 0)
+    lax.fori_loop(0, blocks, greet, 0, unroll=True)
     for table in tables:
         table.start()
     pl.semaphore_wait(barrier, sections * blocks - 1)
@@ -357,8 +357,8 @@
     pltpu.make_async_copy(
         x_ref.at[row_block(sec, ctx)], xbuf.at[sec, ctx], x_recv.at[sec]
     ).start()
-    lax.fori_loop(1, blocks, send_x(sec), 0)
-    lax.fori_loop(0, blocks, send_x(other), 0)
+    lax.fori_loop(1, blocks, send_x(sec), 0, unroll=True)
+    lax.fori_loop(0, blocks, send_x(other), 0, unroll=True)
 
     def send_og(step, carry):
         to_ctx = lax.rem(ctx + step, blocks)
@@ -366,7 +366,7 @@
         return carry
 
     pltpu.make_async_copy(og_ref.at[row_block(sec, ctx)], ogbuf.at[ctx], og_recv).start()
-    lax.fori_loop(1, blocks, send_og, 0)
+    lax.fori_loop(1, blocks, send_og, 0, unroll=True)
 
     tap_load.wait()
     tap_rows[...] = jnp.zeros_like(tap_rows)
@@ -379,6 +379,9 @@
 
     remote(tap_half(other), tbuf.at[sec], t_send, t_recv, other, ctx)
     pltpu.make_async_copy(tap_half(sec), tbuf.at[sec], t_recv).start()
+
+    def rows_at(first):
+        return pl.ds(first if isinstance(first, int) else pl.multiple_of(first, GROUP), GROUP)
 
     def stage_one(blocks_of, first_row):
         cols = jnp.concatenate(
@@ -388,7 +391,7 @@
         out = out.reshape(2, blocks, GROUP, groups * lanes)
         for g in range(groups):
             for part in range(2):
-                ybuf[:, pl.ds(first_row + g * GROUP, GROUP), pl.ds(part * lanes, lanes)] = out[
+                ybuf[:, rows_at(first_row + g * GROUP), pl.ds(part * lanes, lanes)] = out[
                     part, :, :, g * lanes : (g + 1) * lanes
                 ]
 
@@ -415,9 +418,9 @@
 
     def inverse_two(k, operand, slots):
         out = jnp.dot(operand, two_inv_v[k], preferred_element_type=F32).astype(BF16)
-        for slot in range(slots):
+        for position, slot in enumerate(slots):
             for g in range(groups):
-                first = (slot * groups + g) * GROUP
+                first = (position * groups + g) * GROUP
                 for part in range(2):
                     qbuf[slot, part, k, :, pl.ds(g * lanes, lanes)] = out[
                         first : first + GROUP, part * lanes : (part + 1) * lanes
@@ -484,17 +487,18 @@
         lax.fori_loop(0, blocks, body, (zero,) * (TAPS - 1), unroll=2)
 
     mixed_row = sections * rows
-    for layer in range(sections - 1, -1, -1):
+    for layer in (sec, other):
         await_bytes(xbuf.at[layer], x_recv.at[layer])
         features_of(layer)
-        stage_one(lambda g: sig[:, pl.ds(g * GROUP, GROUP), :], mixed_row + layer * rows)
+        first_row = pl.multiple_of(mixed_row + layer * rows, rows)
+        stage_one(lambda g: sig[:, pl.ds(g * GROUP, GROUP), :], first_row)
     tables[2].wait()
     tables[3].wait()
 
     def mixed_point(k):
         mixed = stage_two(k, mixed_row, channels)
         spec[k, pl.ds(mixed_row, channels)] = mixed
-        inverse_two(k, product(spec[k, pl.ds(0, channels)], mixed, False), sections)
+        inverse_two(k, product(spec[k, pl.ds(0, channels)], mixed, False), range(sections))
 
     each_point(mixed_point)
     for layer in range(sections):
@@ -510,6 +514,15 @@
         @pl.when(sec != layer)
         def _():
             remote(src, dst, send_sem, recv_sem, layer, ctx)
+
+    def filter_grad_of(layer):
+        out = inverse_one(1 + layer)
+        for a in range(blocks):
+            for g in range(groups):
+                fgbuf[layer, pl.ds(g * GROUP, GROUP), pl.ds(a * lanes, lanes)] = out[
+                    a, :, g * lanes : (g + 1) * lanes
+                ].astype(BF16)
+        send_home(layer, fgbuf.at[layer], fg_out.at[half(sec)], fg_send, fg_recv)
 
     for layer in range(sections - 1, -1, -1):
         if layer == sections - 1:
@@ -525,9 +538,11 @@
             d_spec = stage_two(k, 0, rows)
             with_h = product(spec[k, pl.ds(layer * rows, rows)], d_spec, True)
             with_w = product(spec[k, pl.ds(mixed_row + layer * rows, rows)], d_spec, True)
-            inverse_two(k, jnp.concatenate([with_h, with_w], axis=0), 2)
+            inverse_two(k, jnp.concatenate([with_h, with_w], axis=0), (0, 1 + layer))
 
         each_point(grad_point)
+        if layer == 0:
+            filter_grad_of(layer)
         out = inverse_one(0)
         for g in range(groups):
             gwbuf[:, pl.ds(g * GROUP, GROUP), :] = out[:, :, g * lanes : (g + 1) * lanes]
@@ -576,16 +591,11 @@
 
             return carry
 
-        lax.fori_loop(0, blocks, send_ig, 0)
-
-        out = inverse_one(1)
-        for a in range(blocks):
-            for g in range(groups):
-                fgbuf[layer, pl.ds(g * GROUP, GROUP), pl.ds(a * lanes, lanes)] = out[
-                    a, :, g * lanes : (g + 1) * lanes
-                ].astype(BF16)
-
-        send_home(layer, fgbuf.at[layer], fg_out.at[half(sec)], fg_send, fg_recv)
+        lax.fori_loop(0, blocks, send_ig, 0, unroll=4)
+
+        if layer == 0:
+            for later in range(1, sections):
+                filter_grad_of(later)
 
     for layer in range(sections - 1, -1, -1):
         for first in range(0, rows, 8):
@@ -621,6 +631,12 @@
     tg_out[...] = tgin[...].T[: 3 * TAPS].reshape(3 * TAPS, 1, channels)
     await_bytes(fg_out, fg_recv)
     await_bytes(ig_out, ig_recv)
+
+
+def write_kernel(ig_ref, fg_ref, tg_ref, ig_out, fg_out, tg_out):
+    ig_out[...] = ig_ref[...]
+    fg_out[...] = fg_ref[...].astype(F32)
+    tg_out[...] = tg_ref[...]
 
 
 def kernel_shards(inputs, out_grad, filters, conv_taps):
@@ -663,7 +679,7 @@
             vmem((blocks, rows, lanes), BF16),
             vmem((blocks, spectrum_rows, 2 * lanes), BF16),
             vmem((blocks, spectrum_rows, 2 * lanes), F32),
-            vmem((2, 2, blocks, GROUP, rows // GROUP * lanes), BF16),
+            vmem((1 + sections, 2, blocks, GROUP, rows // GROUP * lanes), BF16),
             vmem((sections, blocks, rows, lanes), F32),
             vmem((blocks, rows, lanes), F32),
             vmem((sections, 3, blocks, rows, lanes), F32),
@@ -692,8 +708,18 @@
             collective_id=0, has_side_effects=True, vmem_limit_bytes=58 * 2**20
         ),
     )(inputs[0], out_grad, filters[0], taps, *(jnp.asarray(table) for table in tables))
-    tap_grad = tap_sums.reshape(1, 3, TAPS, channels)
-    return (in_grad[None], filter_grad.astype(F32)[None], tap_grad)
+    in_grad, filter_grad, tap_grad = pl.pallas_call(
+        write_kernel,
+        out_shape=(
+            jax.ShapeDtypeStruct(in_grad.shape, BF16),
+            jax.ShapeDtypeStruct(filter_grad.shape, F32),
+            jax.ShapeDtypeStruct(tap_sums.shape, F32),
+        ),
+        in_specs=[vmem_spec] * 3,
+        out_specs=(vmem_spec,) * 3,
+        compiler_params=pltpu.CompilerParams(vmem_limit_bytes=58 * 2**20),
+    )(in_grad, filter_grad, tap_sums)
+    return (in_grad[None], filter_grad[None], tap_grad.reshape(1, 3, TAPS, channels))
 
 
 def solution(mesh):

time: 39 us -> 34.2 us (0.88)
  local copies, waits for them, and re-layouts: 2.97 us -> 0 us
  other arithmetic: 1.78 us -> 0 us
    unnamed x2 -> x0, local copies, waits for them, and re-layouts: 2.97 us -> none
    pallas_call x1, Pallas kernels: 33.4 us -> 31.4 us  [kernel_shards(): pl.pallas_call(functools.partial(mixer_kernel, sections), out_shape=(jax....]
    pallas_call x0 -> x1, Pallas kernels: none -> 1.95 us  [kernel_shards(): pl.pallas_call(write_kernel, out_shape=(jax.ShapeDtypeStruct(in_grad.shap...]
    broadcast_in_dim x1 -> x0, other arithmetic: 1.78 us -> none  [kernel_shards(): return (in_grad[None], filter_grad.astype(F32)[None], tap_grad)]
where the time goes in v2:
time: 34.2 us; the launch traced here: 34 us
  Pallas kernels  33.4 us (98%)
  between operations  0.64 us (2%)
    pallas_call x1, Pallas kernels, kernel_shards(): pl.pallas_call(functools.partial(mixer_kernel, sections), out_shape=(jax....  31.4 us
    pallas_call x1, Pallas kernels, kernel_shards(): pl.pallas_call(write_kernel, out_shape=(jax.ShapeDtypeStruct(in_grad.shap...  1.95 us

profile of v2, /device:TPU:0, one launch (start us, length us, event | category | flops | bytes accessed | tf_op | source)
XLA Modules:
  0.0 34.0 jit_solution(5312696531942855595)
XLA Ops:
  0.6 31.4 %shard_map.103 = (bf16[1024,128]{1,0:T(8,128)(2,1)}, bf16[64,2048]{1,0:T(8,128)(2,1)}, f32[21,1,64]{2,1,0:T(1,128)}) custom-call(bf16[1024,128]{1,0:T(8,128)(2,1)} %bitcast.6, bf16[1024,128]{1,0:T(8,128)(2,1)} %og_ref.1, bf16[64,2048]{1,0:T(8,128)(2,1)} %bitcast.7, f32[21,1,1024]{2,1,0:T(1,128)} %bitcast.8, bf16[512,256]{1,0:T(8,128)(2,1)} %constant.8.clone.one_ref, ...), custom_call_target="tpu_custom_call" | custom-call | tf_op jit(solution)/shard_map/pallas_call | solution.py:656
  32.0 2.0 %shard_map.104 = (bf16[1024,128]{1,0:T(8,128)(2,1)}, f32[64,2048]{1,0:T(8,128)}, f32[21,1,64]{2,1,0:T(1,128)}) custom-call(bf16[1024,128]{1,0:T(8,128)(2,1)} %get-tuple-element.9.ig_ref, bf16[64,2048]{1,0:T(8,128)(2,1)} %get-tuple-element.10.fg_ref, f32[21,1,64]{2,1,0:T(1,128)} %get-tuple-element.11.tg_ref), custom_call_target="tpu_custom_call" | custom-call | tf_op jit(solution)/shard_map/pallas_call | solution.py:711

commit v3 on v2

--- a/solution.py
+++ b/solution.py
@@ -342,8 +342,8 @@
     def await_bytes(ref, sem):
         pltpu.make_async_copy(ref, ref, sem).wait()
 
-    remote(filt_ref.at[half(other)], hbuf.at[sec], h_send, h_recv, other, ctx)
-    pltpu.make_async_copy(filt_ref.at[half(sec)], hbuf.at[sec], h_recv).start()
+    remote(filt_ref.at[half(other)], hbuf.at[sec], h_send, h_recv.at[1], other, ctx)
+    pltpu.make_async_copy(filt_ref.at[half(sec)], hbuf.at[sec], h_recv.at[0]).start()
 
     def send_x(to_sec):
         def send(step, carry):
@@ -377,8 +377,8 @@
         first = lax.rem(tap_first, lanes) + which * rows
         return tap_rows.at[pl.ds(pl.multiple_of(first, rows), rows)]
 
-    remote(tap_half(other), tbuf.at[sec], t_send, t_recv, other, ctx)
-    pltpu.make_async_copy(tap_half(sec), tbuf.at[sec], t_recv).start()
+    remote(tap_half(other), tbuf.at[sec], t_send, t_recv.at[1], other, ctx)
+    pltpu.make_async_copy(tap_half(sec), tbuf.at[sec], t_recv.at[0]).start()
 
     def rows_at(first):
         return pl.ds(first if isinstance(first, int) else pl.multiple_of(first, GROUP), GROUP)
@@ -433,31 +433,6 @@
             preferred_element_type=F32,
         )
         return out.reshape(blocks, GROUP, groups * lanes)
-
-    tables[0].wait()
-    tables[1].wait()
-    await_bytes(hbuf, h_recv)
-    for layer in range(sections):
-        stage_one(
-            lambda g: jnp.stack(
-                [
-                    hbuf[layer, pl.ds(g * GROUP, GROUP), pl.ds(a * lanes, lanes)]
-                    for a in range(blocks)
-                ]
-            ),
-            layer * rows,
-        )
-
-    def filter_point(k):
-        spec[k, pl.ds(0, channels)] = stage_two(k, 0, channels)
-
-    each_point(filter_point)
-
-    await_bytes(tbuf, t_recv)
-    for layer in range(sections):
-        values = tbuf[layer]
-        for n in range(3 * TAPS):
-            tapb[layer, n] = jnp.broadcast_to(values[:, n : n + 1], (rows, lanes))
 
     lane = lax.broadcasted_iota(jnp.int32, (rows, lanes), 1)
 
@@ -486,23 +461,40 @@
         zero = jnp.zeros((rows, lanes), F32)
         lax.fori_loop(0, blocks, body, (zero,) * (TAPS - 1), unroll=2)
 
-    mixed_row = sections * rows
-    for layer in (sec, other):
+    pair = 2 * rows
+    for place, layer in enumerate((sec, other)):
+        first_row = pl.multiple_of(layer * pair, pair)
+        if place == 0:
+            tables[0].wait()
+        await_bytes(hbuf.at[layer], h_recv.at[place])
+        stage_one(
+            lambda g: jnp.stack(
+                [
+                    hbuf[layer, pl.ds(g * GROUP, GROUP), pl.ds(a * lanes, lanes)]
+                    for a in range(blocks)
+                ]
+            ),
+            first_row,
+        )
+        await_bytes(tbuf.at[layer], t_recv.at[place])
+        values = tbuf[layer]
+        for n in range(3 * TAPS):
+            tapb[layer, n] = jnp.broadcast_to(values[:, n : n + 1], (rows, lanes))
         await_bytes(xbuf.at[layer], x_recv.at[layer])
         features_of(layer)
-        first_row = pl.multiple_of(mixed_row + layer * rows, rows)
-        stage_one(lambda g: sig[:, pl.ds(g * GROUP, GROUP), :], first_row)
-    tables[2].wait()
-    tables[3].wait()
-
-    def mixed_point(k):
-        mixed = stage_two(k, mixed_row, channels)
-        spec[k, pl.ds(mixed_row, channels)] = mixed
-        inverse_two(k, product(spec[k, pl.ds(0, channels)], mixed, False), range(sections))
-
-    each_point(mixed_point)
-    for layer in range(sections):
-        out = inverse_one(layer)
+        stage_one(lambda g: sig[:, pl.ds(g * GROUP, GROUP), :], first_row + rows)
+        if place == 0:
+            tables[1].wait()
+            tables[2].wait()
+            tables[3].wait()
+
+        def mixed_point(k):
+            both = stage_two(k, first_row, pair)
+            spec[k, pl.ds(first_row, pair)] = both
+            inverse_two(k, product(both[:rows], both[rows:], False), (0,))
+
+        each_point(mixed_point)
+        out = inverse_one(0)
         for g in range(groups):
             cbuf[layer, :, pl.ds(g * GROUP, GROUP), :] = out[:, :, g * lanes : (g + 1) * lanes]
 
@@ -536,8 +528,8 @@
 
         def grad_point(k):
             d_spec = stage_two(k, 0, rows)
-            with_h = product(spec[k, pl.ds(layer * rows, rows)], d_spec, True)
-            with_w = product(spec[k, pl.ds(mixed_row + layer * rows, rows)], d_spec, True)
+            with_h = product(spec[k, pl.ds(layer * pair, rows)], d_spec, True)
+            with_w = product(spec[k, pl.ds(layer * pair + rows, rows)], d_spec, True)
             inverse_two(k, jnp.concatenate([with_h, with_w], axis=0), (0, 1 + layer))
 
         each_point(grad_point)
@@ -577,21 +569,12 @@
 
         def send_ig(step, carry):
             to_ctx = lax.rem(ctx + step, blocks)
-            src = igbuf.at[layer, to_ctx]
             dst = ig_out.at[row_block(sec, ctx)]
-            local = (sec == layer) & (step == 0)
-
-            @pl.when(local)
-            def _():
-                pltpu.make_async_copy(src, dst, ig_recv).start()
-
-            @pl.when(jnp.logical_not(local))
-            def _():
-                remote(src, dst, ig_send, ig_recv, layer, to_ctx)
-
+            remote(igbuf.at[layer, to_ctx], dst, ig_send, ig_recv, layer, to_ctx)
             return carry
 
-        lax.fori_loop(0, blocks, send_ig, 0, unroll=4)
+        lax.fori_loop(1, blocks, send_ig, 0, unroll=True)
+        send_home(layer, igbuf.at[layer, ctx], ig_out.at[row_block(sec, ctx)], ig_send, ig_recv)
 
         if layer == 0:
             for later in range(1, sections):
@@ -633,10 +616,28 @@
     await_bytes(ig_out, ig_recv)
 
 
-def write_kernel(ig_ref, fg_ref, tg_ref, ig_out, fg_out, tg_out):
-    ig_out[...] = ig_ref[...]
-    fg_out[...] = fg_ref[...].astype(F32)
-    tg_out[...] = tg_ref[...]
+def write_kernel(ig_ref, fg_ref, tg_ref, ig_out, fg_out, tg_out, narrow, wide, sems, load, store):
+    whole = [
+        pltpu.make_async_copy(ig_ref, ig_out, sems.at[0]),
+        pltpu.make_async_copy(tg_ref, tg_out, sems.at[1]),
+    ]
+    parts = [pl.ds(first, GROUP) for first in range(0, fg_ref.shape[0], GROUP)]
+    loads = [
+        pltpu.make_async_copy(fg_ref.at[part], narrow.at[part], load.at[n])
+        for n, part in enumerate(parts)
+    ]
+    stores = [
+        pltpu.make_async_copy(wide.at[part], fg_out.at[part], store.at[n])
+        for n, part in enumerate(parts)
+    ]
+    for copy in loads + whole:
+        copy.start()
+    for n, part in enumerate(parts):
+        loads[n].wait()
+        wide[part] = narrow[part].astype(F32)
+        stores[n].start()
+    for copy in stores + whole:
+        copy.wait()
 
 
 def kernel_shards(inputs, out_grad, filters, conv_taps):
@@ -692,9 +693,9 @@
             dma(()),
             dma(()),
             dma(()),
-            dma(()),
-            dma(()),
-            dma(()),
+            dma((2,)),
+            dma(()),
+            dma((2,)),
             dma(()),
             dma(()),
             dma(()),
@@ -715,8 +716,15 @@
             jax.ShapeDtypeStruct(filter_grad.shape, F32),
             jax.ShapeDtypeStruct(tap_sums.shape, F32),
         ),
-        in_specs=[vmem_spec] * 3,
-        out_specs=(vmem_spec,) * 3,
+        in_specs=[any_spec] * 3,
+        out_specs=(any_spec,) * 3,
+        scratch_shapes=[
+            vmem(filter_grad.shape, BF16),
+            vmem(filter_grad.shape, F32),
+            dma((2,)),
+            dma((channels // GROUP,)),
+            dma((channels // GROUP,)),
+        ],
         compiler_params=pltpu.CompilerParams(vmem_limit_bytes=58 * 2**20),
     )(in_grad, filter_grad, tap_sums)
     return (in_grad[None], filter_grad[None], tap_grad.reshape(1, 3, TAPS, channels))

time: 34.2 us -> 41.4 us (1.21)
  Pallas kernels: 33.4 us -> 40.6 us
    pallas_call x1, Pallas kernels: 1.95 us -> 9.46 us  [kernel_shards(): pl.pallas_call(write_kernel, out_shape=(jax.ShapeDtypeStruct(in_grad.shap...]
where the time goes in v3:
time: 41.4 us; the launch traced here: 41.2 us
  Pallas kernels  40.6 us (98%)
  between operations  0.64 us (2%)
    pallas_call x1, Pallas kernels, kernel_shards(): pl.pallas_call(functools.partial(mixer_kernel, sections), out_shape=(jax....  31.1 us
    pallas_call x1, Pallas kernels, kernel_shards(): pl.pallas_call(write_kernel, out_shape=(jax.ShapeDtypeStruct(in_grad.shap...  9.46 us

profile of v3, /device:TPU:0, one launch (start us, length us, event | category | flops | bytes accessed | tf_op | source)
XLA Modules:
  0.0 41.2 jit_solution(3769897418981900352)
XLA Ops:
  0.6 31.1 %shard_map.103 = (bf16[1024,128]{1,0:T(8,128)(2,1)}, bf16[64,2048]{1,0:T(8,128)(2,1)}, f32[21,1,64]{2,1,0:T(1,128)}) custom-call(bf16[1024,128]{1,0:T(8,128)(2,1)} %bitcast.6, bf16[1024,128]{1,0:T(8,128)(2,1)} %og_ref.1, bf16[64,2048]{1,0:T(8,128)(2,1)} %bitcast.7, f32[21,1,1024]{2,1,0:T(1,128)} %bitcast.8, bf16[512,256]{1,0:T(8,128)(2,1)} %constant.8.clone.one_ref, ...), custom_call_target="tpu_custom_call" | custom-call | tf_op jit(solution)/shard_map/pallas_call | solution.py:657
  31.8 9.5 %shard_map.104 = (bf16[1024,128]{1,0:T(8,128)(2,1)}, f32[64,2048]{1,0:T(8,128)}, f32[21,1,64]{2,1,0:T(1,128)}) custom-call(bf16[1024,128]{1,0:T(8,128)(2,1)} %get-tuple-element.9.ig_ref, bf16[64,2048]{1,0:T(8,128)(2,1)} %get-tuple-element.10.fg_ref, f32[21,1,64]{2,1,0:T(1,128)} %get-tuple-element.11.tg_ref), custom_call_target="tpu_custom_call" | custom-call | tf_op jit(solution)/shard_map/pallas_call | solution.py:712

commit v4 on v3

--- a/solution.py
+++ b/solution.py
@@ -233,9 +233,9 @@
 
 def mixer_kernel(
     sections,
-    x_ref,
-    og_ref,
-    filt_ref,
+    x_hbm,
+    og_hbm,
+    filt_hbm,
     tap_ref,
     one_ref,
     one_inv_ref,
@@ -244,6 +244,9 @@
     ig_out,
     fg_out,
     tg_out,
+    x_ref,
+    og_ref,
+    filt_ref,
     xbuf,
     ogbuf,
     hbuf,
@@ -284,6 +287,7 @@
     tg_recv,
     table_sem,
     blk_sem,
+    load_sem,
 ):
     sec = lax.axis_index("section")
     ctx = lax.axis_index("ctx")
@@ -305,6 +309,13 @@
     tap_lane = pl.multiple_of(tap_first // lanes * lanes, lanes)
     tap_load = pltpu.make_async_copy(tap_ref.at[:, :, pl.ds(tap_lane, lanes)], tap_blk, blk_sem)
     tap_load.start()
+
+    loads = [
+        pltpu.make_async_copy(src, dst, load_sem.at[n])
+        for n, (src, dst) in enumerate(((filt_hbm, filt_ref), (x_hbm, x_ref), (og_hbm, og_ref)))
+    ]
+    for load in loads:
+        load.start()
 
     barrier = pltpu.get_barrier_semaphore()
 
@@ -342,6 +353,7 @@
     def await_bytes(ref, sem):
         pltpu.make_async_copy(ref, ref, sem).wait()
 
+    loads[0].wait()
     remote(filt_ref.at[half(other)], hbuf.at[sec], h_send, h_recv.at[1], other, ctx)
     pltpu.make_async_copy(filt_ref.at[half(sec)], hbuf.at[sec], h_recv.at[0]).start()
 
@@ -354,6 +366,7 @@
 
         return send
 
+    loads[1].wait()
     pltpu.make_async_copy(
         x_ref.at[row_block(sec, ctx)], xbuf.at[sec, ctx], x_recv.at[sec]
     ).start()
@@ -365,6 +378,7 @@
         remote(og_ref.at[row_block(sec, to_ctx)], ogbuf.at[ctx], og_send, og_recv, sec, to_ctx)
         return carry
 
+    loads[2].wait()
     pltpu.make_async_copy(og_ref.at[row_block(sec, ctx)], ogbuf.at[ctx], og_recv).start()
     lax.fori_loop(1, blocks, send_og, 0, unroll=True)
 
@@ -616,28 +630,10 @@
     await_bytes(ig_out, ig_recv)
 
 
-def write_kernel(ig_ref, fg_ref, tg_ref, ig_out, fg_out, tg_out, narrow, wide, sems, load, store):
-    whole = [
-        pltpu.make_async_copy(ig_ref, ig_out, sems.at[0]),
-        pltpu.make_async_copy(tg_ref, tg_out, sems.at[1]),
-    ]
-    parts = [pl.ds(first, GROUP) for first in range(0, fg_ref.shape[0], GROUP)]
-    loads = [
-        pltpu.make_async_copy(fg_ref.at[part], narrow.at[part], load.at[n])
-        for n, part in enumerate(parts)
-    ]
-    stores = [
-        pltpu.make_async_copy(wide.at[part], fg_out.at[part], store.at[n])
-        for n, part in enumerate(parts)
-    ]
-    for copy in loads + whole:
-        copy.start()
-    for n, part in enumerate(parts):
-        loads[n].wait()
-        wide[part] = narrow[part].astype(F32)
-        stores[n].start()
-    for copy in stores + whole:
-        copy.wait()
+def write_kernel(ig_ref, fg_ref, tg_ref, ig_out, fg_out, tg_out):
+    ig_out[...] = ig_ref[...]
+    fg_out[...] = fg_ref[...].astype(F32)
+    tg_out[...] = tg_ref[...]
 
 
 def kernel_shards(inputs, out_grad, filters, conv_taps):
@@ -664,6 +660,9 @@
         in_specs=[hbm_spec] * 8,
         out_specs=(any_spec, any_spec, vmem_spec),
         scratch_shapes=[
+            vmem((depth, lanes), BF16),
+            vmem((depth, lanes), BF16),
+            vmem((channels, length), BF16),
             vmem((sections, blocks, rows, lanes), BF16),
             vmem((blocks, rows, lanes), BF16),
             vmem((sections, rows, length), BF16),
@@ -704,6 +703,7 @@
             dma(()),
             dma((4,)),
             dma(()),
+            dma((3,)),
         ],
         compiler_params=pltpu.CompilerParams(
             collective_id=0, has_side_effects=True, vmem_limit_bytes=58 * 2**20
@@ -716,15 +716,8 @@
             jax.ShapeDtypeStruct(filter_grad.shape, F32),
             jax.ShapeDtypeStruct(tap_sums.shape, F32),
         ),
-        in_specs=[any_spec] * 3,
-        out_specs=(any_spec,) * 3,
-        scratch_shapes=[
-            vmem(filter_grad.shape, BF16),
-            vmem(filter_grad.shape, F32),
-            dma((2,)),
-            dma((channels // GROUP,)),
-            dma((channels // GROUP,)),
-        ],
+        in_specs=[vmem_spec] * 3,
+        out_specs=(vmem_spec,) * 3,
         compiler_params=pltpu.CompilerParams(vmem_limit_bytes=58 * 2**20),
     )(in_grad, filter_grad, tap_sums)
     return (in_grad[None], filter_grad[None], tap_grad.reshape(1, 3, TAPS, channels))

time: 41.4 us -> 33.9 us (0.82)
  Pallas kernels: 40.6 us -> 33.1 us
    pallas_call x1, Pallas kernels: 9.46 us -> 1.95 us  [kernel_shards(): pl.pallas_call(write_kernel, out_shape=(jax.ShapeDtypeStruct(in_grad.shap...]
where the time goes in v4:
time: 33.9 us; the launch traced here: 33.7 us
  Pallas kernels  33.1 us (98%)
  between operations  0.64 us (2%)
    pallas_call x1, Pallas kernels, kernel_shards(): pl.pallas_call(functools.partial(mixer_kernel, sections), out_shape=(jax....  31.1 us
    pallas_call x1, Pallas kernels, kernel_shards(): pl.pallas_call(write_kernel, out_shape=(jax.ShapeDtypeStruct(in_grad.shap...  1.95 us

profile of v4, /device:TPU:0, one launch (start us, length us, event | category | flops | bytes accessed | tf_op | source)
XLA Modules:
  0.0 33.7 jit_solution(1666009849644449174)
XLA Ops:
  0.6 31.1 %shard_map.103 = (bf16[1024,128]{1,0:T(8,128)(2,1)}, bf16[64,2048]{1,0:T(8,128)(2,1)}, f32[21,1,64]{2,1,0:T(1,128)}) custom-call(bf16[1024,128]{1,0:T(8,128)(2,1)} %bitcast.6, bf16[1024,128]{1,0:T(8,128)(2,1)} %og_hbm.1, bf16[64,2048]{1,0:T(8,128)(2,1)} %bitcast.7, f32[21,1,1024]{2,1,0:T(1,128)} %bitcast.8, bf16[512,256]{1,0:T(8,128)(2,1)} %constant.8.clone.one_ref, ...), custom_call_target="tpu_custom_call" | custom-call | tf_op jit(solution)/shard_map/pallas_call | solution.py:653
  31.8 2.0 %shard_map.104 = (bf16[1024,128]{1,0:T(8,128)(2,1)}, f32[64,2048]{1,0:T(8,128)}, f32[21,1,64]{2,1,0:T(1,128)}) custom-call(bf16[1024,128]{1,0:T(8,128)(2,1)} %get-tuple-element.9.ig_ref, bf16[64,2048]{1,0:T(8,128)(2,1)} %get-tuple-element.10.fg_ref, f32[21,1,64]{2,1,0:T(1,128)} %get-tuple-element.11.tg_ref), custom_call_target="tpu_custom_call" | custom-call | tf_op jit(solution)/shard_map/pallas_call | solution.py:712

commit v5 on v4

--- a/solution.py
+++ b/solution.py
@@ -207,6 +207,7 @@
 
 TAPS = 7
 GROUP = 16
+CHUNK = 4
 MESH = pl.DeviceIdType.MESH
 F32 = jnp.float32
 BF16 = jnp.bfloat16
@@ -217,18 +218,20 @@
     first_k = np.arange(blocks_a)
     phase_one = 2 * np.pi * np.outer(first_k + 0.25, np.arange(blocks_a)) / blocks_a
     one = np.stack([np.cos(phase_one), -np.sin(phase_one)])
-    first = np.einsum("rka,cd->rkcad", one, np.eye(GROUP))
+    first = np.einsum("rka,cd->krcad", one, np.eye(GROUP))
     first = first.reshape(2 * blocks_a * GROUP, blocks_a * GROUP)
-    points = first_k[:, None, None] + 0.25 + blocks_a * np.arange(block_b)[None, None, :]
-    phase_two = 2 * np.pi * np.arange(block_b)[None, :, None] * points / total_n
+    phase_turn = 2 * np.pi * np.outer(first_k + 0.25, np.arange(block_b)) / total_n
+    turn = np.stack([np.cos(phase_turn), -np.sin(phase_turn)])
+    turn = np.repeat(turn[:, :, None, :], GROUP, axis=2).astype(np.float32)
+    phase_two = 2 * np.pi * np.outer(np.arange(block_b), np.arange(block_b)) / block_b
     real, imag = np.cos(phase_two), -np.sin(phase_two)
     second = np.concatenate(
-        [np.concatenate([real, imag], axis=2), np.concatenate([-imag, real], axis=2)], axis=1
-    )
-    return tuple(
-        array.astype(ml_dtypes.bfloat16)
-        for array in (first, first.T / total_n, second, second.transpose(0, 2, 1))
-    )
+        [np.concatenate([real, imag], axis=1), np.concatenate([-imag, real], axis=1)], axis=0
+    )
+    rounded = [
+        array.astype(ml_dtypes.bfloat16) for array in (first, first.T / total_n, second, second.T)
+    ]
+    return (*rounded, turn)
 
 
 def mixer_kernel(
@@ -241,6 +244,7 @@
     one_inv_ref,
     two_ref,
     two_inv_ref,
+    turn_ref,
     ig_out,
     fg_out,
     tg_out,
@@ -257,6 +261,7 @@
     one_inv_v,
     two_v,
     two_inv_v,
+    turn_v,
     tapb,
     xs_ref,
     feat,
@@ -300,7 +305,7 @@
     tables = [
         pltpu.make_async_copy(src, dst, table_sem.at[n])
         for n, (src, dst) in enumerate(
-            ((one_ref, one_v), (two_ref, two_v), (one_inv_ref, one_inv_v), (two_inv_ref, two_inv_v))
+            ((one_ref, one_v), (two_ref, two_v), (one_inv_ref, one_inv_v), (two_inv_ref, two_inv_v), (turn_ref, turn_v))
         )
     ]
 
@@ -397,48 +402,64 @@
     def rows_at(first):
         return pl.ds(first if isinstance(first, int) else pl.multiple_of(first, GROUP), GROUP)
 
+    chunk_size = min(CHUNK, blocks)
+
+    def each_chunk(body):
+        def step(n, carry):
+            body(pl.ds(n * chunk_size, chunk_size))
+            return carry
+
+        lax.fori_loop(0, blocks // chunk_size, step, 0, unroll=True)
+
     def stage_one(blocks_of, first_row):
         cols = jnp.concatenate(
             [blocks_of(g).reshape(blocks * GROUP, lanes) for g in range(groups)], axis=1
         )
-        out = jnp.dot(one_v[...], cols, preferred_element_type=F32).astype(BF16)
-        out = out.reshape(2, blocks, GROUP, groups * lanes)
-        for g in range(groups):
-            for part in range(2):
-                ybuf[:, rows_at(first_row + g * GROUP), pl.ds(part * lanes, lanes)] = out[
-                    part, :, :, g * lanes : (g + 1) * lanes
-                ]
-
-    def stage_two(k, first_row, count):
-        return jnp.dot(ybuf[k, pl.ds(first_row, count)], two_v[k], preferred_element_type=F32)
-
-    def each_point(body):
-        def step(k, carry):
-            body(k)
-            return carry
-
-        lax.fori_loop(0, blocks, step, 0, unroll=True)
+
+        def chunk(ks):
+            out = jnp.dot(
+                one_v[pl.ds(ks.start * 2 * GROUP, ks.size * 2 * GROUP)],
+                cols,
+                preferred_element_type=F32,
+            ).reshape(ks.size, 2, GROUP, groups * lanes)
+            turn_r, turn_i = turn_v[0, ks], turn_v[1, ks]
+            for g in range(groups):
+                real = out[:, 0, :, g * lanes : (g + 1) * lanes]
+                imag = out[:, 1, :, g * lanes : (g + 1) * lanes]
+                where = rows_at(first_row + g * GROUP)
+                ybuf[ks, where, pl.ds(0, lanes)] = (real * turn_r - imag * turn_i).astype(BF16)
+                ybuf[ks, where, pl.ds(lanes, lanes)] = (real * turn_i + imag * turn_r).astype(BF16)
+
+        each_chunk(chunk)
+
+    def stage_two(ks, first_row, count):
+        operand = ybuf[ks, pl.ds(first_row, count)].reshape(ks.size * count, 2 * lanes)
+        out = jnp.dot(operand, two_v[...], preferred_element_type=F32)
+        return out.reshape(ks.size, count, 2 * lanes)
 
     def product(left, right, conj):
-        left_r, left_i = left[:, :lanes], left[:, lanes:]
-        right_r, right_i = right[:, :lanes], right[:, lanes:]
+        left_r, left_i = left[..., :lanes], left[..., lanes:]
+        right_r, right_i = right[..., :lanes], right[..., lanes:]
         if conj:
             real = left_r * right_r + left_i * right_i
             imag = left_r * right_i - left_i * right_r
         else:
             real = left_r * right_r - left_i * right_i
             imag = left_r * right_i + left_i * right_r
-        return jnp.concatenate([real, imag], axis=1).astype(BF16)
-
-    def inverse_two(k, operand, slots):
-        out = jnp.dot(operand, two_inv_v[k], preferred_element_type=F32).astype(BF16)
-        for position, slot in enumerate(slots):
-            for g in range(groups):
-                first = (position * groups + g) * GROUP
-                for part in range(2):
-                    qbuf[slot, part, k, :, pl.ds(g * lanes, lanes)] = out[
-                        first : first + GROUP, part * lanes : (part + 1) * lanes
-                    ]
+        return jnp.concatenate([real, imag], axis=2).astype(BF16)
+
+    def inverse_two(ks, operand, slot):
+        count = operand.shape[1]
+        out = jnp.dot(
+            operand.reshape(ks.size * count, 2 * lanes), two_inv_v[...], preferred_element_type=F32
+        ).reshape(ks.size, count, 2 * lanes)
+        turn_r, turn_i = turn_v[0, ks], turn_v[1, ks]
+        for g in range(groups):
+            real = out[:, g * GROUP : (g + 1) * GROUP, :lanes]
+            imag = out[:, g * GROUP : (g + 1) * GROUP, lanes:]
+            where = pl.ds(g * lanes, lanes)
+            qbuf[slot, ks, 0, :, where] = (real * turn_r + imag * turn_i).astype(BF16)
+            qbuf[slot, ks, 1, :, where] = (imag * turn_r - real * turn_i).astype(BF16)
 
     def inverse_one(slot):
         out = jnp.dot(
@@ -480,6 +501,7 @@
         first_row = pl.multiple_of(layer * pair, pair)
         if place == 0:
             tables[0].wait()
+            tables[4].wait()
         await_bytes(hbuf.at[layer], h_recv.at[place])
         stage_one(
             lambda g: jnp.stack(
@@ -502,12 +524,12 @@
             tables[2].wait()
             tables[3].wait()
 
-        def mixed_point(k):
-            both = stage_two(k, first_row, pair)
-            spec[k, pl.ds(first_row, pair)] = both
-            inverse_two(k, product(both[:rows], both[rows:], False), (0,))
-
-        each_point(mixed_point)
+        def mixed_points(ks):
+            both = stage_two(ks, first_row, pair)
+            spec[ks, pl.ds(first_row, pair)] = both
+            inverse_two(ks, product(both[:, :rows], both[:, rows:], False), 0)
+
+        each_chunk(mixed_points)
         out = inverse_one(0)
         for g in range(groups):
             cbuf[layer, :, pl.ds(g * GROUP, GROUP), :] = out[:, :, g * lanes : (g + 1) * lanes]
@@ -540,13 +562,14 @@
         sig[...] = (carried[...].astype(F32) * feat[layer, 0].astype(F32)).astype(BF16)
         stage_one(lambda g: sig[:, pl.ds(g * GROUP, GROUP), :], 0)
 
-        def grad_point(k):
-            d_spec = stage_two(k, 0, rows)
-            with_h = product(spec[k, pl.ds(layer * pair, rows)], d_spec, True)
-            with_w = product(spec[k, pl.ds(layer * pair + rows, rows)], d_spec, True)
-            inverse_two(k, jnp.concatenate([with_h, with_w], axis=0), (0, 1 + layer))
-
-        each_point(grad_point)
+        def grad_points(ks):
+            d_spec = stage_two(ks, 0, rows)
+            with_h = product(spec[ks, pl.ds(layer * pair, rows)], d_spec, True)
+            with_w = product(spec[ks, pl.ds(layer * pair + rows, rows)], d_spec, True)
+            inverse_two(ks, with_h, 0)
+            inverse_two(ks, with_w, 1 + layer)
+
+        each_chunk(grad_points)
         if layer == 0:
             filter_grad_of(layer)
         out = inverse_one(0)
@@ -657,7 +680,7 @@
             jax.ShapeDtypeStruct((channels, length), BF16),
             jax.ShapeDtypeStruct((3 * TAPS, 1, channels), F32),
         ),
-        in_specs=[hbm_spec] * 8,
+        in_specs=[hbm_spec] * 9,
         out_specs=(any_spec, any_spec, vmem_spec),
         scratch_shapes=[
             vmem((depth, lanes), BF16),
@@ -673,13 +696,14 @@
             vmem(tables[1].shape, BF16),
             vmem(tables[2].shape, BF16),
             vmem(tables[3].shape, BF16),
+            vmem(tables[4].shape, F32),
             vmem((sections, 3 * TAPS, rows, lanes), F32),
             vmem((sections, TAPS, blocks, rows, lanes), F32),
             vmem((sections, 3, blocks, rows, lanes), BF16),
             vmem((blocks, rows, lanes), BF16),
             vmem((blocks, spectrum_rows, 2 * lanes), BF16),
             vmem((blocks, spectrum_rows, 2 * lanes), F32),
-            vmem((1 + sections, 2, blocks, GROUP, rows // GROUP * lanes), BF16),
+            vmem((1 + sections, blocks, 2, GROUP, rows // GROUP * lanes), BF16),
             vmem((sections, blocks, rows, lanes), F32),
             vmem((blocks, rows, lanes), F32),
             vmem((sections, 3, blocks, rows, lanes), F32),
@@ -701,7 +725,7 @@
             dma(()),
             dma(()),
             dma(()),
-            dma((4,)),
+            dma((5,)),
             dma(()),
             dma((3,)),
         ],

time: 33.9 us -> 33.5 us (0.988)
  Pallas kernels: 33.1 us -> 32.7 us
    pallas_call x1, Pallas kernels: 31.1 us -> 30.8 us  [kernel_shards(): pl.pallas_call(functools.partial(mixer_kernel, sections), out_shape=(jax....]
where the time goes in v5:
time: 33.5 us; the launch traced here: 33.4 us
  Pallas kernels  32.7 us (98%)
  between operations  0.64 us (2%)
    pallas_call x1, Pallas kernels, kernel_shards(): pl.pallas_call(functools.partial(mixer_kernel, sections), out_shape=(jax....  30.8 us
    pallas_call x1, Pallas kernels, kernel_shards(): pl.pallas_call(write_kernel, out_shape=(jax.ShapeDtypeStruct(in_grad.shap...  1.95 us

profile of v5, /device:TPU:0, one launch (start us, length us, event | category | flops | bytes accessed | tf_op | source)
XLA Modules:
  0.0 33.4 jit_solution(3311610546533190947)
XLA Ops:
  0.6 30.8 %shard_map.112 = (bf16[1024,128]{1,0:T(8,128)(2,1)}, bf16[64,2048]{1,0:T(8,128)(2,1)}, f32[21,1,64]{2,1,0:T(1,128)}) custom-call(bf16[1024,128]{1,0:T(8,128)(2,1)} %bitcast.6, bf16[1024,128]{1,0:T(8,128)(2,1)} %og_hbm.1, bf16[64,2048]{1,0:T(8,128)(2,1)} %bitcast.7, f32[21,1,1024]{2,1,0:T(1,128)} %bitcast.8, bf16[512,256]{1,0:T(8,128)(2,1)} %constant.10.clone.one_ref, ...), custom_call_target="tpu_custom_call" | custom-call | tf_op jit(solution)/shard_map/pallas_call | solution.py:676
  31.4 2.0 %shard_map.113 = (bf16[1024,128]{1,0:T(8,128)(2,1)}, f32[64,2048]{1,0:T(8,128)}, f32[21,1,64]{2,1,0:T(1,128)}) custom-call(bf16[1024,128]{1,0:T(8,128)(2,1)} %get-tuple-element.9.ig_ref, bf16[64,2048]{1,0:T(8,128)(2,1)} %get-tuple-element.10.fg_ref, f32[21,1,64]{2,1,0:T(1,128)} %get-tuple-element.11.tg_ref), custom_call_target="tpu_custom_call" | custom-call | tf_op jit(solution)/shard_map/pallas_call | solution.py:736

commit v6 on v5

--- a/solution.py
+++ b/solution.py
@@ -362,9 +362,12 @@
     remote(filt_ref.at[half(other)], hbuf.at[sec], h_send, h_recv.at[1], other, ctx)
     pltpu.make_async_copy(filt_ref.at[half(sec)], hbuf.at[sec], h_recv.at[0]).start()
 
+    def partner(step):
+        return lax.rem(ctx + 1 + lax.rem(ctx * max(1, blocks // 4) + step, blocks - 1), blocks)
+
     def send_x(to_sec):
         def send(step, carry):
-            to_ctx = lax.rem(ctx + step, blocks)
+            to_ctx = partner(step)
             src = x_ref.at[row_block(to_sec, to_ctx)]
             remote(src, xbuf.at[sec, ctx], x_send, x_recv.at[sec], to_sec, to_ctx)
             return carry
@@ -375,17 +378,20 @@
     pltpu.make_async_copy(
         x_ref.at[row_block(sec, ctx)], xbuf.at[sec, ctx], x_recv.at[sec]
     ).start()
-    lax.fori_loop(1, blocks, send_x(sec), 0, unroll=True)
-    lax.fori_loop(0, blocks, send_x(other), 0, unroll=True)
+    lax.fori_loop(0, blocks - 1, send_x(sec), 0, unroll=True)
+    lax.fori_loop(0, blocks - 1, send_x(other), 0, unroll=True)
+    remote(
+        x_ref.at[row_block(other, ctx)], xbuf.at[sec, ctx], x_send, x_recv.at[sec], other, ctx
+    )
 
     def send_og(step, carry):
-        to_ctx = lax.rem(ctx + step, blocks)
+        to_ctx = partner(step)
         remote(og_ref.at[row_block(sec, to_ctx)], ogbuf.at[ctx], og_send, og_recv, sec, to_ctx)
         return carry
 
     loads[2].wait()
     pltpu.make_async_copy(og_ref.at[row_block(sec, ctx)], ogbuf.at[ctx], og_recv).start()
-    lax.fori_loop(1, blocks, send_og, 0, unroll=True)
+    lax.fori_loop(0, blocks - 1, send_og, 0, unroll=True)
 
     tap_load.wait()
     tap_rows[...] = jnp.zeros_like(tap_rows)
@@ -605,12 +611,12 @@
         lax.fori_loop(0, blocks, transposed_at, (zero,) * (TAPS - 1), unroll=2)
 
         def send_ig(step, carry):
-            to_ctx = lax.rem(ctx + step, blocks)
+            to_ctx = partner(step)
             dst = ig_out.at[row_block(sec, ctx)]
             remote(igbuf.at[layer, to_ctx], dst, ig_send, ig_recv, layer, to_ctx)
             return carry
 
-        lax.fori_loop(1, blocks, send_ig, 0, unroll=True)
+        lax.fori_loop(0, blocks - 1, send_ig, 0, unroll=True)
         send_home(layer, igbuf.at[layer, ctx], ig_out.at[row_block(sec, ctx)], ig_send, ig_recv)
 
         if layer == 0:

time: 33.5 us -> 33.9 us (1.012)
  Pallas kernels: 32.7 us -> 33.1 us
    pallas_call x1, Pallas kernels: 30.8 us -> 31.1 us  [kernel_shards(): pl.pallas_call(functools.partial(mixer_kernel, sections), out_shape=(jax....]
where the time goes in v6:
time: 33.9 us; the launch traced here: 33.7 us
  Pallas kernels  33.1 us (98%)
  between operations  0.64 us (2%)
    pallas_call x1, Pallas kernels, kernel_shards(): pl.pallas_call(functools.partial(mixer_kernel, sections), out_shape=(jax....  31.1 us
    pallas_call x1, Pallas kernels, kernel_shards(): pl.pallas_call(write_kernel, out_shape=(jax.ShapeDtypeStruct(in_grad.shap...  1.95 us

profile of v6, /device:TPU:0, one launch (start us, length us, event | category | flops | bytes accessed | tf_op | source)
XLA Modules:
  0.0 33.7 jit_solution(4743397854968763128)
XLA Ops:
  0.6 31.1 %shard_map.112 = (bf16[1024,128]{1,0:T(8,128)(2,1)}, bf16[64,2048]{1,0:T(8,128)(2,1)}, f32[21,1,64]{2,1,0:T(1,128)}) custom-call(bf16[1024,128]{1,0:T(8,128)(2,1)} %bitcast.6, bf16[1024,128]{1,0:T(8,128)(2,1)} %og_hbm.1, bf16[64,2048]{1,0:T(8,128)(2,1)} %bitcast.7, f32[21,1,1024]{2,1,0:T(1,128)} %bitcast.8, bf16[512,256]{1,0:T(8,128)(2,1)} %constant.10.clone.one_ref, ...), custom_call_target="tpu_custom_call" | custom-call | tf_op jit(solution)/shard_map/pallas_call | solution.py:682
  31.8 2.0 %shard_map.113 = (bf16[1024,128]{1,0:T(8,128)(2,1)}, f32[64,2048]{1,0:T(8,128)}, f32[21,1,64]{2,1,0:T(1,128)}) custom-call(bf16[1024,128]{1,0:T(8,128)(2,1)} %get-tuple-element.9.ig_ref, bf16[64,2048]{1,0:T(8,128)(2,1)} %get-tuple-element.10.fg_ref, f32[21,1,64]{2,1,0:T(1,128)} %get-tuple-element.11.tg_ref), custom_call_target="tpu_custom_call" | custom-call | tf_op jit(solution)/shard_map/pallas_call | solution.py:742

commit v7 on v5

--- a/solution.py
+++ b/solution.py
@@ -494,7 +494,7 @@
             return tuple(rolled)
 
         zero = jnp.zeros((rows, lanes), F32)
-        lax.fori_loop(0, blocks, body, (zero,) * (TAPS - 1), unroll=2)
+        lax.fori_loop(0, blocks, body, (zero,) * (TAPS - 1), unroll=4)
 
     pair = 2 * rows
     for place, layer in enumerate((sec, other)):
@@ -602,7 +602,7 @@
             return tuple(rolled)
 
         zero = jnp.zeros((rows, lanes), F32)
-        lax.fori_loop(0, blocks, transposed_at, (zero,) * (TAPS - 1), unroll=2)
+        lax.fori_loop(0, blocks, transposed_at, (zero,) * (TAPS - 1), unroll=4)
 
         def send_ig(step, carry):
             to_ctx = lax.rem(ctx + step, blocks)
@@ -629,7 +629,7 @@
                 return tuple(new)
 
             zero_8 = jnp.zeros((8, lanes), F32)
-            sums = lax.fori_loop(0, blocks, add_taps, (zero_8,) * (3 * TAPS), unroll=4)
+            sums = lax.fori_loop(0, blocks, add_taps, (zero_8,) * (3 * TAPS), unroll=True)
             lane_8 = lax.broadcasted_iota(jnp.int32, (8, lanes), 1)
             packed = zero_8
             for j in range(TAPS):

time: 33.5 us -> 32.9 us (0.982)
  Pallas kernels: 32.7 us -> 32.2 us
    pallas_call x1, Pallas kernels: 30.8 us -> 30.2 us  [kernel_shards(): pl.pallas_call(functools.partial(mixer_kernel, sections), out_shape=(jax....]
where the time goes in v7:
time: 32.9 us; the launch traced here: 32.8 us
  Pallas kernels  32.2 us (98%)
  between operations  0.64 us (2%)
    pallas_call x1, Pallas kernels, kernel_shards(): pl.pallas_call(functools.partial(mixer_kernel, sections), out_shape=(jax....  30.2 us
    pallas_call x1, Pallas kernels, kernel_shards(): pl.pallas_call(write_kernel, out_shape=(jax.ShapeDtypeStruct(in_grad.shap...  1.95 us

profile of v7, /device:TPU:0, one launch (start us, length us, event | category | flops | bytes accessed | tf_op | source)
XLA Modules:
  0.0 32.8 jit_solution(1938199250006973096)
XLA Ops:
  0.6 30.2 %shard_map.112 = (bf16[1024,128]{1,0:T(8,128)(2,1)}, bf16[64,2048]{1,0:T(8,128)(2,1)}, f32[21,1,64]{2,1,0:T(1,128)}) custom-call(bf16[1024,128]{1,0:T(8,128)(2,1)} %bitcast.6, bf16[1024,128]{1,0:T(8,128)(2,1)} %og_hbm.1, bf16[64,2048]{1,0:T(8,128)(2,1)} %bitcast.7, f32[21,1,1024]{2,1,0:T(1,128)} %bitcast.8, bf16[512,256]{1,0:T(8,128)(2,1)} %constant.10.clone.one_ref, ...), custom_call_target="tpu_custom_call" | custom-call | tf_op jit(solution)/shard_map/pallas_call | solution.py:676
  30.8 2.0 %shard_map.113 = (bf16[1024,128]{1,0:T(8,128)(2,1)}, f32[64,2048]{1,0:T(8,128)}, f32[21,1,64]{2,1,0:T(1,128)}) custom-call(bf16[1024,128]{1,0:T(8,128)(2,1)} %get-tuple-element.9.ig_ref, bf16[64,2048]{1,0:T(8,128)(2,1)} %get-tuple-element.10.fg_ref, f32[21,1,64]{2,1,0:T(1,128)} %get-tuple-element.11.tg_ref), custom_call_target="tpu_custom_call" | custom-call | tf_op jit(solution)/shard_map/pallas_call | solution.py:736

commit v8 on v7

--- a/solution.py
+++ b/solution.py
@@ -494,7 +494,7 @@
             return tuple(rolled)
 
         zero = jnp.zeros((rows, lanes), F32)
-        lax.fori_loop(0, blocks, body, (zero,) * (TAPS - 1), unroll=4)
+        lax.fori_loop(0, blocks, body, (zero,) * (TAPS - 1), unroll=True)
 
     pair = 2 * rows
     for place, layer in enumerate((sec, other)):
@@ -602,7 +602,7 @@
             return tuple(rolled)
 
         zero = jnp.zeros((rows, lanes), F32)
-        lax.fori_loop(0, blocks, transposed_at, (zero,) * (TAPS - 1), unroll=4)
+        lax.fori_loop(0, blocks, transposed_at, (zero,) * (TAPS - 1), unroll=True)
 
         def send_ig(step, carry):
             to_ctx = lax.rem(ctx + step, blocks)

time: 32.9 us -> 32.8 us (level)
  no operation moved by 1% of the time
where the time goes in v8:
time: 32.8 us; the launch traced here: 32.6 us
  Pallas kernels  32 us (98%)
  between operations  0.64 us (2%)
    pallas_call x1, Pallas kernels, kernel_shards(): pl.pallas_call(functools.partial(mixer_kernel, sections), out_shape=(jax....  30 us
    pallas_call x1, Pallas kernels, kernel_shards(): pl.pallas_call(write_kernel, out_shape=(jax.ShapeDtypeStruct(in_grad.shap...  1.95 us

profile of v8, /device:TPU:0, one launch (start us, length us, event | category | flops | bytes accessed | tf_op | source)
XLA Modules:
  0.0 32.6 jit_solution(16725152247265687363)
XLA Ops:
  0.6 30.0 %shard_map.112 = (bf16[1024,128]{1,0:T(8,128)(2,1)}, bf16[64,2048]{1,0:T(8,128)(2,1)}, f32[21,1,64]{2,1,0:T(1,128)}) custom-call(bf16[1024,128]{1,0:T(8,128)(2,1)} %bitcast.6, bf16[1024,128]{1,0:T(8,128)(2,1)} %og_hbm.1, bf16[64,2048]{1,0:T(8,128)(2,1)} %bitcast.7, f32[21,1,1024]{2,1,0:T(1,128)} %bitcast.8, bf16[512,256]{1,0:T(8,128)(2,1)} %constant.10.clone.one_ref, ...), custom_call_target="tpu_custom_call" | custom-call | tf_op jit(solution)/shard_map/pallas_call | solution.py:676
  30.7 2.0 %shard_map.113 = (bf16[1024,128]{1,0:T(8,128)(2,1)}, f32[64,2048]{1,0:T(8,128)}, f32[21,1,64]{2,1,0:T(1,128)}) custom-call(bf16[1024,128]{1,0:T(8,128)(2,1)} %get-tuple-element.9.ig_ref, bf16[64,2048]{1,0:T(8,128)(2,1)} %get-tuple-element.10.fg_ref, f32[21,1,64]{2,1,0:T(1,128)} %get-tuple-element.11.tg_ref), custom_call_target="tpu_custom_call" | custom-call | tf_op jit(solution)/shard_map/pallas_call | solution.py:736
